TPU v7x, 32 devices: a whole 2x2x4 slice. The times are simulated.
32 devices in a mesh: section: 4 (over x, core), rows: 8 (over z, y).
Axes of the slice: x: 2, y: 2, z: 4, core: 2. Of those that a mesh axis runs over, the one named last changes fastest.
Arguments:
- fwd_in: bfloat16 [4, 128, 32, 512], P('section', 'rows'), may hold values from -6 to 6
- grad_in: bfloat16 [4, 128, 32, 512], P('section', 'rows'), may hold values from -6 to 6
- saved_in: bfloat16 [4, 128, 32, 512], P('section', 'rows'), may hold values from -6 to 6
- mirror_held: bfloat16 [4, 128, 32, 512], P('section', 'rows'), may hold values from -6 to 6
- target: bfloat16 [128, 32, 512], P('rows'), may hold values from -6 to 6
- w_first: bfloat16 [4, 3, 3, 512, 512], P('section'), may hold values from -0.09375 to 0.09375
- w_second: bfloat16 [4, 3, 3, 512, 512], P('section'), may hold values from -0.09375 to 0.09375
Outputs:
- fwd_next: bfloat16 [4, 128, 32, 512], P('section', 'rows')
- grad_next: bfloat16 [4, 128, 32, 512], P('section', 'rows')
- mirror_next: bfloat16 [4, 128, 32, 512], P('section', 'rows')
All inputs are finite; a program needn't handle non-finite values.
Results may differ from a plain program's by a relative error of at most 0.0085.
Values may be sent and summed in bfloat16 or wider, within the bound.
A program may use at most 64 MiB of HBM per device.

v0:
```python
import jax
import jax.numpy as jnp
from jax import lax
from jax.sharding import PartitionSpec as P


def extended(value, sides, width):
    for axis, dim in sides:
        count, length = (lax.axis_size(axis), value.shape[dim])
        up = [(i, (i + 1) % count) for i in range(count - 1)]
        down = [(j, i) for i, j in up]
        last = lax.slice_in_dim(value, length - width, length, axis=dim)
        leading = lax.slice_in_dim(value, 0, width, axis=dim)
        before = lax.ppermute(last, axis, up)
        after = lax.ppermute(leading, axis, down)
        value = jnp.concatenate([before, value, after], axis=dim)
    return value


def shifted(value, axis, by):
    count = lax.axis_size(axis)
    pairs = [(i, i + by) for i in range(count) if 0 <= i + by < count]
    return lax.ppermute(value, axis, pairs)


def conv_rows(field, kernel):
    return lax.conv_general_dilated(
        field,
        kernel,
        (1, 1),
        ((0, 0), (1, 1)),
        dimension_numbers=("NHWC", "HWIO", "NHWC"),
        preferred_element_type=jnp.float32,
    )


def flipped(kernel):
    return jnp.transpose(kernel[::-1, ::-1], (0, 1, 3, 2))


def silu_slope(pre):
    sig = jax.nn.sigmoid(pre)
    return sig * (1.0 + pre * (1.0 - sig))


def double_rim(field):
    return extended(field, (("rows", 1),), 2)


def on_device(fwd_in, grad_in, saved_in, mirror_held, target, w_first, w_second):
    act = fwd_in[0]
    grad = grad_in[0]
    saved = saved_in[0]
    held = mirror_held[0]
    kern_one = w_first[0]
    kern_two = w_second[0]
    local_rows = act.shape[0]
    section = lax.axis_index("section")
    sections = lax.axis_size("section")
    decoder = (section >= sections // 2).astype(jnp.float32)
    is_last = section == sections - 1
    first_row = lax.axis_index("rows") * local_rows
    total_rows = local_rows * lax.axis_size("rows")
    global_row = first_row - 1 + jnp.arange(local_rows + 2, dtype=jnp.int32)
    inside = ((global_row >= 0) & (global_row < total_rows)).astype(jnp.float32)[:, None, None]
    flip_one = flipped(kern_one)
    flip_two = flipped(kern_two)
    block_in = act.astype(jnp.float32) + decoder * held.astype(jnp.float32)
    block_b = block_in.astype(jnp.bfloat16)
    padded = double_rim(block_b[None])
    hidden = (jax.nn.silu(conv_rows(padded, kern_one)[0]) * inside).astype(jnp.bfloat16)
    output = (block_in + conv_rows(hidden[None], kern_two)[0]).astype(jnp.bfloat16)
    g_top = jnp.where(
        is_last,
        output.astype(jnp.float32) - target.astype(jnp.float32),
        grad.astype(jnp.float32) + (1.0 - decoder) * held.astype(jnp.float32),
    ).astype(jnp.bfloat16)
    kept = jnp.where(is_last, block_b, saved)
    paired = jnp.stack([kept, g_top], axis=0)
    rimmed = double_rim(paired)
    pre = conv_rows(rimmed[0:1], kern_one)[0]
    back = conv_rows(rimmed[1:2], flip_two)[0]
    g_mid = (silu_slope(pre) * back * inside).astype(jnp.bfloat16)
    g_low = (g_top.astype(jnp.float32) + conv_rows(g_mid[None], flip_one)[0]).astype(jnp.bfloat16)
    fwd_next = shifted(output, "section", 1)
    grad_next = shifted(g_low, "section", -1)
    payload = jnp.where(section >= sections // 2, g_low, output)
    spread = lax.all_to_all(payload[None], "section", split_axis=2, concat_axis=0, tiled=True)
    payload = lax.all_to_all(spread[::-1], "section", split_axis=0, concat_axis=2, tiled=True)[0]
    return (fwd_next[None], grad_next[None], payload[None])


def solution(mesh):
    return jax.shard_map(
        on_device,
        mesh=mesh,
        in_specs=(
            P("section", "rows", None, None),
            P("section", "rows", None, None),
            P("section", "rows", None, None),
            P("section", "rows", None, None),
            P("rows", None, None),
            P("section", None, None, None, None),
            P("section", None, None, None, None),
        ),
        out_specs=(
            P("section", "rows", None, None),
            P("section", "rows", None, None),
            P("section", "rows", None, None),
        ),
        check_vma=False,
    )
```

profile of v0, /device:TPU:0, one launch (start us, length us, event | category | flops | bytes accessed | tf_op | source)
XLA Modules:
  0.0 79.5 jit_solution(12865706994303850779)
XLA Ops:
  0.6 2.2 %copy_select_fusion = (bf16[1,16,32,512]{3,1,2,0:T(8,128)(2,1)S(1)}, bf16[1,16,32,512]{3,1,2,0:T(8,128)(2,1)S(1)}) fusion(bf16[1,16,32,512]{3,2,1,0:T(8,128)(2,1)} %param.9, pred[]{:T(512)S(6)} %eq.3, bf16[1,16,32,512]{3,2,1,0:T(8,128)(2,1)} %param.10, f32[]{:T(128)S(6)} %convert_element_type.57, bf16[1,16,32,512]{3,2,1,0:T(8,128)(2,1)} %param.7), kind=kLoop, calls=%fused_computation.80 | loop fusion | flops 1572864 | bytes 2621445 | tf_op jit(solution)/shard_map/jit(_where)/select_n | solution.py:78
  2.9 0.1 fusion.109
  3.0 4.9 %collective-permute-start = (bf16[1,2,32,512]{3,1,2,0:T(2,128)(2,1)S(1)}, bf16[1,2,32,512]{3,1,2,0:T(2,128)(2,1)S(1)}, u32[]{:S(2)}, u32[]{:S(2)}) collective-permute-start(bf16[1,2,32,512]{3,1,2,0:T(2,128)(2,1)S(1)} %get-tuple-element.23), channel_id=1, source_target_pairs={{0,1},{1,2},{2,3},{3,4},{4,5},{5,6},{6,7},{8,9},{9,10},{10,11},{11... | collective-permute-start | bytes 196616 | tf_op jit(solution)/shard_map/ppermute | solution.py:14
  7.9 1.3 %collective-permute-start.1 = (bf16[1,2,32,512]{3,1,2,0:T(2,128)(2,1)S(1)}, bf16[1,2,32,512]{3,1,2,0:T(2,128)(2,1)S(1)}, u32[]{:S(2)}, u32[]{:S(2)}) collective-permute-start(bf16[1,2,32,512]{3,1,2,0:T(2,128)(2,1)S(1)} %get-tuple-element.24), channel_id=1, source_target_pairs={{1,0},{2,1},{3,2},{4,3},{5,4},{6,5},{7,6},{9,8},{10,9},{11,10},{12... | collective-permute-start | bytes 196616 | tf_op jit(solution)/shard_map/ppermute | solution.py:15
  9.2 0.6 collective-permute-done
  9.8 4.3 %collective-permute-done.1 = bf16[1,2,32,512]{3,1,2,0:T(2,128)(2,1)S(1)} collective-permute-done((bf16[1,2,32,512]{3,1,2,0:T(2,128)(2,1)S(1)}, bf16[1,2,32,512]{3,1,2,0:T(2,128)(2,1)S(1)}, u32[]{:S(2)}, u32[]{:S(2)}) %collective-permute-start.1) | collective-permute-done | bytes 65568 | tf_op jit(solution)/shard_map/ppermute | solution.py:15
  14.0 0.0 copy-start.4
  14.0 0.4 maximum_bitcast_fusion
  14.5 0.1 pad
  14.5 0.0 copy-start.5
  14.6 0.2 copy.29
  14.8 0.0 slice-start
  14.8 0.1 slice.35
  14.9 1.5 %copy-done.4 = bf16[1,3,3,512,512]{4,3,2,1,0:T(8,128)(2,1)S(1)} copy-done((bf16[1,3,3,512,512]{4,3,2,1,0:T(8,128)(2,1)S(1)}, bf16[1,3,3,512,512]{4,3,2,1,0:T(8,128)(2,1)}, u32[]{:S(2)}) %copy-start.4) | copy-done | bytes 4718616
  16.4 0.0 copy-done.5
  16.4 0.0 slice-start.1
  16.4 3.9 %fusion.30 = bf16[18,1,8,5,512]{4,2,3,0,1:T(8,128)(2,1)S(1)} fusion(bf16[1,3,3,512,512]{4,3,2,1,0:T(8,128)(2,1)S(1)} %copy-done.4, bf16[20,1,7,2,512]{4,2,3,0,1:T(8,128)(2,1)S(1)} %slice.35, bf16[20,1,8,5,512]{4,2,3,0,1:T(8,128)(2,1)S(1)} %copy.29, f32[18]{0:T(128)S(1)} %and_convert_fusion, pred[8,5]{0,1:T(8,128)(4,1)S(1)} %copy-done.5), kind=kOutput, calls=%fused_computation.28 | convolution fusion | flops 3403776000 | bytes 6561904 | tf_op jit(solution)/shard_map/conv_general_dilated | solution.py:27
  20.3 0.0 slice-done
  20.3 0.0 slice-done.1
  20.3 3.2 %fusion.2 = f32[16,8,5,512]{3,1,2,0:T(8,128)S(1)} fusion(bf16[1,3,3,512,512]{4,3,2,1,0:T(8,128)(2,1)S(1)} %bitcast.110, bf16[18,1,7,1,512]{4,2,3,0,1:T(8,128)(2,1)S(1)} %get-tuple-element.22, bf16[18,1,7,1,512]{4,2,3,0,1:T(8,128)(2,1)S(1)} %get-tuple-element.21, bf16[18,1,8,5,512]{4,2,3,0,1:T(8,128)(2,1)S(1)} %fusion.30), kind=kOutput, calls=%fused_computation.2 | convolution fusion | flops 3025059840 | bytes 7024640 | tf_op jit(solution)/shard_map/conv_general_dilated | solution.py:27
  23.6 0.0 copy-start
  23.6 0.0 copy-start.1
  23.6 0.0 copy-start.2
  23.6 0.0 copy-start.3
  23.6 0.8 copy.30
  24.4 0.2 copy-done
  24.6 0.2 copy-done.1
  24.8 0.2 copy-done.2
  24.9 0.2 copy-done.3
  25.1 1.4 %fusion.55 = (bf16[16,32,512]{2,0,1:T(8,128)(2,1)S(1)}, bf16[16,32,512]{2,0,1:T(8,128)(2,1)S(1)}) fusion(bf16[1,16,32,512]{3,2,1,0:T(8,128)(2,1)S(1)} %copy-done.2, bf16[16,32,512]{2,1,0:T(8,128)(2,1)S(1)} %copy-done.3, f32[]{:T(128)S(6)} %sub.15, pred[]{:T(512)S(6)} %eq.3, bf16[1,16,32,512]{3,2,1,0:T(8,128)(2,1)S(1)} %copy-done, ...), kind=kLoop, calls=%fused_computation.48 | loop fusion | flops 3670016 | bytes 4194313 | tf_op jit(solution)/shard_map/convert_element_type | solution.py:77
  26.5 0.2 pad_maximum_fusion.2
  26.7 4.3 %collective-permute-start.3 = (bf16[2,2,32,512]{3,1,2,0:T(2,128)(2,1)S(1)}, bf16[2,2,32,512]{3,1,2,0:T(2,128)(2,1)S(1)}, u32[]{:S(2)}, u32[]{:S(2)}) collective-permute-start(bf16[2,2,32,512]{3,1,2,0:T(2,128)(2,1)S(1)} %get-tuple-element.17), channel_id=1, source_target_pairs={{0,1},{1,2},{2,3},{3,4},{4,5},{5,6},{6,7},{8,9},{9,10},{10,11},{11... | collective-permute-start | bytes 393224 | tf_op jit(solution)/shard_map/ppermute | solution.py:14
  31.1 1.5 %collective-permute-start.4 = (bf16[2,2,32,512]{3,1,2,0:T(2,128)(2,1)S(1)}, bf16[2,2,32,512]{3,1,2,0:T(2,128)(2,1)S(1)}, u32[]{:S(2)}, u32[]{:S(2)}) collective-permute-start(bf16[2,2,32,512]{3,1,2,0:T(2,128)(2,1)S(1)} %get-tuple-element.18), channel_id=1, source_target_pairs={{1,0},{2,1},{3,2},{4,3},{5,4},{6,5},{7,6},{9,8},{10,9},{11,10},{12... | collective-permute-start | bytes 393224 | tf_op jit(solution)/shard_map/ppermute | solution.py:15
  32.5 2.4 %collective-permute-done.3 = bf16[2,2,32,512]{3,1,2,0:T(2,128)(2,1)S(1)} collective-permute-done((bf16[2,2,32,512]{3,1,2,0:T(2,128)(2,1)S(1)}, bf16[2,2,32,512]{3,1,2,0:T(2,128)(2,1)S(1)}, u32[]{:S(2)}, u32[]{:S(2)}) %collective-permute-start.3) | collective-permute-done | bytes 131104 | tf_op jit(solution)/shard_map/ppermute | solution.py:14
  34.9 3.0 %collective-permute-done.4 = bf16[2,2,32,512]{3,1,2,0:T(2,128)(2,1)S(1)} collective-permute-done((bf16[2,2,32,512]{3,1,2,0:T(2,128)(2,1)S(1)}, bf16[2,2,32,512]{3,1,2,0:T(2,128)(2,1)S(1)}, u32[]{:S(2)}, u32[]{:S(2)}) %collective-permute-start.4) | collective-permute-done | bytes 131104 | tf_op jit(solution)/shard_map/ppermute | solution.py:15
  37.9 1.1 %pad_maximum_fusion = bf16[2,20,32,512]{3,1,2,0:T(8,128)(2,1)S(1)} fusion(bf16[2,2,32,512]{3,1,2,0:T(2,128)(2,1)S(1)} %collective-permute-done.4, bf16[1,16,32,512]{3,1,2,0:T(8,128)(2,1)S(1)} %bitcast.98, bf16[1,16,32,512]{3,1,2,0:T(8,128)(2,1)S(1)} %get-tuple-element.11, bf16[2,2,32,512]{3,1,2,0:T(2,128)(2,1)S(1)} %collective-permute-done.3), kind=kLoop, calls=%fused_computation.20 | loop fusion | flops 5242880 | bytes 2621440 | tf_op jit(solution)/shard_map/concatenate | solution.py:16
  39.0 0.1 slice_bitcast_fusion.3
  39.1 0.1 pad.6
  39.2 0.2 copy.37
  39.5 0.1 slice.42
  39.6 3.7 %fusion = f32[18,8,5,512]{3,1,2,0:T(8,128)S(1)} fusion(bf16[1,3,3,512,512]{4,3,2,1,0:T(8,128)(2,1)S(1)} %bitcast.110, bf16[20,1,7,2,512]{4,2,3,0,1:T(8,128)(2,1)S(1)} %slice.42, bf16[20,1,8,5,512]{4,2,3,0,1:T(8,128)(2,1)S(1)} %copy.37), kind=kOutput, calls=%fused_computation | convolution fusion | flops 3400826880 | bytes 7299072 | tf_op jit(solution)/shard_map/conv_general_dilated | solution.py:27
  43.2 0.1 pad.4
  43.3 0.2 copy.35
  43.6 0.1 slice.40
  43.7 4.1 %fusion.27 = bf16[18,1,8,5,512]{4,2,3,0,1:T(8,128)(2,1)S(1)} fusion(f32[18,8,5,512]{3,1,2,0:T(8,128)S(1)} %fusion, bf16[1,3,3,512,512]{4,3,2,1,0:T(8,128)(2,1)S(1)} %copy-done.4, bf16[20,1,7,2,512]{4,2,3,0,1:T(8,128)(2,1)S(1)} %slice.40, bf16[20,1,8,5,512]{4,2,3,0,1:T(8,128)(2,1)S(1)} %copy.35, f32[18]{0:T(128)S(1)} %and_convert_fusion, ...), kind=kOutput, calls=%fused_computation.27 | convolution fusion | flops 3405619200 | bytes 8036464 | tf_op jit(solution)/shard_map/conv_general_dilated | solution.py:27
  47.8 3.3 %fusion.4 = f32[16,8,5,512]{3,1,2,0:T(8,128)S(1)} fusion(bf16[1,3,3,512,512]{4,3,2,1,0:T(8,128)(2,1)S(1)} %copy-done.4, bf16[18,1,7,1,512]{4,2,3,0,1:T(8,128)(2,1)S(1)} %get-tuple-element.20, bf16[18,1,7,1,512]{4,2,3,0,1:T(8,128)(2,1)S(1)} %get-tuple-element.19, bf16[18,1,8,5,512]{4,2,3,0,1:T(8,128)(2,1)S(1)} %fusion.27), kind=kOutput, calls=%fused_computation.4 | convolution fusion | flops 3025059840 | bytes 7024640 | tf_op jit(solution)/shard_map/conv_general_dilated | solution.py:27
  51.1 0.8 copy.38
  51.9 1.1 %select_bitcast_fusion = (bf16[1,16,32,512]{3,1,0,2:T(8,128)(2,1)}, bf16[16,32,512]{2,0,1:T(8,128)(2,1)S(1)}) fusion(bf16[16,32,512]{2,0,1:T(8,128)(2,1)S(1)} %get-tuple-element.14, pred[]{:T(512)S(6)} %ge.11, f32[16,1,40,512]{3,0,2,1:T(8,128)S(1)} %bitcast.100, bf16[16,32,512]{2,0,1:T(8,128)(2,1)S(1)} %get-tuple-element.13), kind=kLoop, calls=%fused_computation.81 | loop fusion | flops 1048576 | bytes 3145729 | tf_op jit(solution)/shard_map/broadcast_in_dim | solution.py:88
  53.0 3.5 %all-to-all-start = ((bf16[1,16,32,512]{3,1,0,2:T(8,128)(2,1)}), bf16[1,16,32,512]{3,1,0,2:T(8,128)(2,1)S(1)}, u32[]{:S(2)}, u32[]{:S(2)}) async-start(bf16[1,16,32,512]{3,1,0,2:T(8,128)(2,1)} %get-tuple-element.9), calls=%async_computation | async-start | bytes 1048576 | tf_op jit(solution)/shard_map/all_to_all | solution.py:88
  56.5 2.4 %collective-permute-start.2 = (bf16[16,32,512]{2,0,1:T(8,128)(2,1)S(1)}, bf16[16,32,512]{2,0,1:T(8,128)(2,1)S(1)}, u32[]{:S(2)}, u32[]{:S(2)}) collective-permute-start(bf16[16,32,512]{2,0,1:T(8,128)(2,1)S(1)} %get-tuple-element.14), channel_id=1, source_target_pairs={{0,8},{8,16},{16,24},{1,9},{9,17},{17,25},{2,10},{10,18},{18,26},{... | collective-permute-start | bytes 1572872 | tf_op jit(solution)/shard_map/ppermute | solution.py:23
  58.9 1.3 %collective-permute-start.5 = (bf16[16,32,512]{2,0,1:T(8,128)(2,1)S(1)}, bf16[16,32,512]{2,0,1:T(8,128)(2,1)S(1)}, u32[]{:S(2)}, u32[]{:S(2)}) collective-permute-start(bf16[16,32,512]{2,0,1:T(8,128)(2,1)S(1)} %get-tuple-element.10), channel_id=1, source_target_pairs={{8,0},{16,8},{24,16},{9,1},{17,9},{25,17},{10,2},{18,10},{26,18},{... | collective-permute-start | bytes 1572872 | tf_op jit(solution)/shard_map/ppermute | solution.py:23
  60.2 5.1 %all-to-all-done = bf16[1,16,32,512]{3,1,0,2:T(8,128)(2,1)S(1)} async-done(((bf16[1,16,32,512]{3,1,0,2:T(8,128)(2,1)}), bf16[1,16,32,512]{3,1,0,2:T(8,128)(2,1)S(1)}, u32[]{:S(2)}, u32[]{:S(2)}) %all-to-all-start) | async-done | bytes 524320 | tf_op jit(solution)/shard_map/all_to_all | solution.py:88
  65.3 0.8 %rev.8 = bf16[4,16,8,512]{3,1,2,0:T(8,128)(2,1)} reverse(bf16[4,16,8,512]{3,1,2,0:T(8,128)(2,1)S(1)} %bitcast.105), dimensions={0} | reverse | bytes 1048576 | tf_op jit(solution)/shard_map/rev | solution.py:89
  66.1 3.5 %all-to-all-start.1 = ((bf16[4,16,8,512]{3,1,2,0:T(8,128)(2,1)}), bf16[4,16,8,512]{3,1,2,0:T(8,128)(2,1)S(1)}, u32[]{:S(2)}, u32[]{:S(2)}) async-start(bf16[4,16,8,512]{3,1,2,0:T(8,128)(2,1)} %rev.8), calls=%async_computation.1 | async-start | bytes 1048576 | tf_op jit(solution)/shard_map/all_to_all | solution.py:89
  69.6 0.0 collective-permute-done.2
  69.6 1.1 %copy.41 = bf16[1,16,32,512]{3,2,1,0:T(8,128)(2,1)} copy(bf16[1,16,32,512]{3,1,2,0:T(8,128)(2,1)S(1)} %bitcast.107) | data formatting | bytes 1048576
  70.7 0.0 collective-permute-done.5
  70.7 1.1 %copy.42 = bf16[1,16,32,512]{3,2,1,0:T(8,128)(2,1)} copy(bf16[1,16,32,512]{3,1,2,0:T(8,128)(2,1)S(1)} %bitcast.106) | data formatting | bytes 1048576
  71.8 6.6 %all-to-all-done.1 = bf16[4,16,8,512]{3,1,2,0:T(8,128)(2,1)S(1)} async-done(((bf16[4,16,8,512]{3,1,2,0:T(8,128)(2,1)}), bf16[4,16,8,512]{3,1,2,0:T(8,128)(2,1)S(1)}, u32[]{:S(2)}, u32[]{:S(2)}) %all-to-all-start.1) | async-done | bytes 524320 | tf_op jit(solution)/shard_map/all_to_all | solution.py:89
  78.4 1.1 %copy.56 = bf16[1,16,4,8,512]{4,3,2,1,0:T(8,128)(2,1)} copy(bf16[1,16,4,8,512]{4,1,3,2,0:T(8,128)(2,1)S(1)} %bitcast.104) | data formatting | bytes 1048576 | tf_op jit(solution)/shard_map/all_to_all | solution.py:89
  (4 shorter events, 0.1 us)
Async XLA Ops:
  3.0 6.8 %collective-permute-start = (bf16[1,2,32,512]{3,1,2,0:T(2,128)(2,1)S(1)}, bf16[1,2,32,512]{3,1,2,0:T(2,128)(2,1)S(1)}, u32[]{:S(2)}, u32[]{:S(2)}) collective-permute-start(bf16[1,2,32,512]{3,1,2,0:T(2,128)(2,1)S(1)} %get-tuple-element.23), channel_id=1, source_target_pairs={{0,1},{1,2},{2,3},{3,4},{4,5},{5,6},{6,7},{8,9},{9,10},{10,11},{11... | collective-permute-start | bytes 196616 | tf_op jit(solution)/shard_map/ppermute | solution.py:14
  7.9 6.2 %collective-permute-start.1 = (bf16[1,2,32,512]{3,1,2,0:T(2,128)(2,1)S(1)}, bf16[1,2,32,512]{3,1,2,0:T(2,128)(2,1)S(1)}, u32[]{:S(2)}, u32[]{:S(2)}) collective-permute-start(bf16[1,2,32,512]{3,1,2,0:T(2,128)(2,1)S(1)} %get-tuple-element.24), channel_id=1, source_target_pairs={{1,0},{2,1},{3,2},{4,3},{5,4},{6,5},{7,6},{9,8},{10,9},{11,10},{12... | collective-permute-start | bytes 196616 | tf_op jit(solution)/shard_map/ppermute | solution.py:15
  14.0 2.3 %copy-start.4 = (bf16[1,3,3,512,512]{4,3,2,1,0:T(8,128)(2,1)S(1)}, bf16[1,3,3,512,512]{4,3,2,1,0:T(8,128)(2,1)}, u32[]{:S(2)}) copy-start(bf16[1,3,3,512,512]{4,3,2,1,0:T(8,128)(2,1)} %param.12) | copy-start | bytes 14155780
  14.5 1.8 %copy-start.5 = (pred[8,5]{0,1:T(8,128)(4,1)S(1)}, pred[8,5]{0,1:T(8,128)(4,1)}, u32[]{:S(2)}) copy-start(pred[8,5]{0,1:T(8,128)(4,1)} %constant.50) | copy-start | bytes 124
  14.8 5.5 %slice-start = ((s8[4718592]{0:T(1024)(128)(4,1)}), s8[4194304]{0:T(1024)(128)(4,1)S(1)}, s32[]{:S(2)}) async-start(s8[4718592]{0:T(1024)(128)(4,1)} %bitcast.109), calls=%async_computation.2 | async-start | bytes 8388608
  16.4 3.9 %slice-start.1 = ((s8[4718592]{0:T(1024)(128)(4,1)}), s8[524288]{0:T(1024)(128)(4,1)S(1)}, s32[]{:S(2)}) async-start(s8[4718592]{0:T(1024)(128)(4,1)} %bitcast.109), calls=%async_computation.3 | async-start | bytes 1048576
  23.6 1.0 %copy-start = (bf16[1,16,32,512]{3,2,1,0:T(8,128)(2,1)S(1)}, bf16[1,16,32,512]{3,2,1,0:T(8,128)(2,1)}, u32[]{:S(2)}) copy-start(bf16[1,16,32,512]{3,2,1,0:T(8,128)(2,1)} %param.10) | copy-start | bytes 1572868
  23.6 1.2 %copy-start.1 = (bf16[1,16,32,512]{3,2,1,0:T(8,128)(2,1)S(1)}, bf16[1,16,32,512]{3,2,1,0:T(8,128)(2,1)}, u32[]{:S(2)}) copy-start(bf16[1,16,32,512]{3,2,1,0:T(8,128)(2,1)} %param.7) | copy-start | bytes 1572868
  23.6 1.3 %copy-start.2 = (bf16[1,16,32,512]{3,2,1,0:T(8,128)(2,1)S(1)}, bf16[1,16,32,512]{3,2,1,0:T(8,128)(2,1)}, u32[]{:S(2)}) copy-start(bf16[1,16,32,512]{3,2,1,0:T(8,128)(2,1)} %param.8) | copy-start | bytes 1572868
  23.6 1.5 %copy-start.3 = (bf16[16,32,512]{2,1,0:T(8,128)(2,1)S(1)}, bf16[16,32,512]{2,1,0:T(8,128)(2,1)}, u32[]{:S(2)}) copy-start(bf16[16,32,512]{2,1,0:T(8,128)(2,1)} %param.11) | copy-start | bytes 1572868
  26.7 8.2 %collective-permute-start.3 = (bf16[2,2,32,512]{3,1,2,0:T(2,128)(2,1)S(1)}, bf16[2,2,32,512]{3,1,2,0:T(2,128)(2,1)S(1)}, u32[]{:S(2)}, u32[]{:S(2)}) collective-permute-start(bf16[2,2,32,512]{3,1,2,0:T(2,128)(2,1)S(1)} %get-tuple-element.17), channel_id=1, source_target_pairs={{0,1},{1,2},{2,3},{3,4},{4,5},{5,6},{6,7},{8,9},{9,10},{10,11},{11... | collective-permute-start | bytes 393224 | tf_op jit(solution)/shard_map/ppermute | solution.py:14
  31.1 6.9 %collective-permute-start.4 = (bf16[2,2,32,512]{3,1,2,0:T(2,128)(2,1)S(1)}, bf16[2,2,32,512]{3,1,2,0:T(2,128)(2,1)S(1)}, u32[]{:S(2)}, u32[]{:S(2)}) collective-permute-start(bf16[2,2,32,512]{3,1,2,0:T(2,128)(2,1)S(1)} %get-tuple-element.18), channel_id=1, source_target_pairs={{1,0},{2,1},{3,2},{4,3},{5,4},{6,5},{7,6},{9,8},{10,9},{11,10},{12... | collective-permute-start | bytes 393224 | tf_op jit(solution)/shard_map/ppermute | solution.py:15
  53.0 12.3 %all-to-all-start = ((bf16[1,16,32,512]{3,1,0,2:T(8,128)(2,1)}), bf16[1,16,32,512]{3,1,0,2:T(8,128)(2,1)S(1)}, u32[]{:S(2)}, u32[]{:S(2)}) async-start(bf16[1,16,32,512]{3,1,0,2:T(8,128)(2,1)} %get-tuple-element.9), calls=%async_computation | async-start | bytes 1048576 | tf_op jit(solution)/shard_map/all_to_all | solution.py:88
  56.5 13.1 %collective-permute-start.2 = (bf16[16,32,512]{2,0,1:T(8,128)(2,1)S(1)}, bf16[16,32,512]{2,0,1:T(8,128)(2,1)S(1)}, u32[]{:S(2)}, u32[]{:S(2)}) collective-permute-start(bf16[16,32,512]{2,0,1:T(8,128)(2,1)S(1)} %get-tuple-element.14), channel_id=1, source_target_pairs={{0,8},{8,16},{16,24},{1,9},{9,17},{17,25},{2,10},{10,18},{18,26},{... | collective-permute-start | bytes 1572872 | tf_op jit(solution)/shard_map/ppermute | solution.py:23
  58.9 11.8 %collective-permute-start.5 = (bf16[16,32,512]{2,0,1:T(8,128)(2,1)S(1)}, bf16[16,32,512]{2,0,1:T(8,128)(2,1)S(1)}, u32[]{:S(2)}, u32[]{:S(2)}) collective-permute-start(bf16[16,32,512]{2,0,1:T(8,128)(2,1)S(1)} %get-tuple-element.10), channel_id=1, source_target_pairs={{8,0},{16,8},{24,16},{9,1},{17,9},{25,17},{10,2},{18,10},{26,18},{... | collective-permute-start | bytes 1572872 | tf_op jit(solution)/shard_map/ppermute | solution.py:23
  66.1 12.3 %all-to-all-start.1 = ((bf16[4,16,8,512]{3,1,2,0:T(8,128)(2,1)}), bf16[4,16,8,512]{3,1,2,0:T(8,128)(2,1)S(1)}, u32[]{:S(2)}, u32[]{:S(2)}) async-start(bf16[4,16,8,512]{3,1,2,0:T(8,128)(2,1)} %rev.8), calls=%async_computation.1 | async-start | bytes 1048576 | tf_op jit(solution)/shard_map/all_to_all | solution.py:89
where the time goes:
time: 79.9 us; the launch traced here: 79.5 us
  starting transfers between devices  22.6 us (28%)
  waiting for transfers between devices  22 us (28%)
  matrix products  18.2 us (23%)
  local copies, waits for them, and re-layouts  9.28 us (12%)
  other arithmetic  6.52 us (8%)
  between operations  0.97 us (1%)
    conv_general_dilated x5, matrix products, conv_rows(): lax.conv_general_dilated(field, kernel, (1, 1), ((0, 0), (1, 1)), dimensi...  18.2 us
    ppermute x2, starting transfers between devices, extended(): before = lax.ppermute(last, axis, up)  9.21 us
    ppermute x2, waiting for transfers between devices, extended(): after = lax.ppermute(leading, axis, down)  7.27 us
    all_to_all x1, waiting for transfers between devices, on_device(): lax.all_to_all(spread[::-1], 'section', split_axis=0, concat_axis=2, tile...  6.62 us
    all_to_all x1, waiting for transfers between devices, on_device(): lax.all_to_all(payload[None], 'section', split_axis=2, concat_axis=0, til...  5.11 us
    unnamed x18, local copies, waits for them, and re-layouts  4.38 us
    ppermute x2, starting transfers between devices, shifted(): return lax.ppermute(value, axis, pairs)  3.69 us
    all_to_all x1, starting transfers between devices, on_device(): lax.all_to_all(payload[None], 'section', split_axis=2, concat_axis=0, til...  3.47 us
  transfers between devices with their start and end apart: 8, of which 6 were waited for; matrix products, arithmetic and copies ran while one was open for 4% of the time, Pallas kernels for 0%

commit v1 on v0

v1 whole, which is shorter than its diff:
```python
import functools

import jax
import jax.numpy as jnp
from jax import lax
from jax.experimental import pallas as pl
from jax.experimental.pallas import tpu as pltpu
from jax.sharding import PartitionSpec as P

MESH = pl.DeviceIdType.MESH
U, KEPT, GTOP, HID, GMID = range(5)
FWD, GRAD, MIRROR = range(3)


def relay_kernel(
    sections, row_devices, width, halves,
    act_hbm, grad_hbm, saved_hbm, held_hbm, target_hbm, w1_hbm, w2_hbm,
    fwd_out, grad_out, mirror_out,
    act, grad, held, target, w1, w2, field, slope, y, low, zeros,
    in_sem, halo_send, halo_recv, out_send, out_recv, local_sem,
):
    size, channels = act.shape
    part = channels // halves
    section = lax.axis_index("section")
    row = lax.axis_index("rows")
    half_sections = sections // 2
    decoder = section >= half_sections
    is_last = section == sections - 1
    dec = decoder.astype(jnp.float32)
    has_up, has_down = row > 0, row < row_devices - 1
    has_prev, has_next = section > 0, section < sections - 1
    mirror = sections - 1 - section
    middle_enc = section == half_sections - 1
    middle_dec = section == half_sections
    middle = jnp.logical_or(middle_enc, middle_dec)
    encoder = jnp.logical_not(decoder)
    inner_dec = jnp.logical_and(decoder, jnp.logical_not(is_last))
    others = jnp.logical_not(inner_dec)
    not_last = jnp.logical_not(is_last)
    at_up = (section, row - 1)
    at_down = (section, row + 1)
    at_prev = (section - 1, row)
    at_next = (section + 1, row)
    at_mirror = (mirror, row)

    inner = pl.ds(width, size)

    def load(src, dst, k):
        return pltpu.make_async_copy(src, dst, in_sem.at[k])

    load_act = load(act_hbm, act, 0)
    load_held = load(held_hbm, held, 1)
    load_grad = load(grad_hbm, grad, 2)
    load_saved = load(saved_hbm, field.at[KEPT, inner], 3)
    load_target = load(target_hbm, target, 4)
    load_w1 = load(w1_hbm, w1, 5)
    load_w2 = load(w2_hbm, w2, 6)
    for copy in (load_act, load_held, load_grad, load_saved, load_w1, load_target, load_w2):
        copy.start()

    barrier = pltpu.get_barrier_semaphore()
    partners = ((has_up, at_up), (has_down, at_down), (has_prev, at_prev), (has_next, at_next))
    count = jnp.int32(1)
    for cond, where in partners:
        @pl.when(cond)
        def _(where=where):
            pl.semaphore_signal(barrier, inc=1, device_id=where, device_id_type=MESH)
        count = count + cond.astype(jnp.int32)
    pl.semaphore_signal(barrier, inc=1, device_id=at_mirror, device_id_type=MESH)

    for k in range(5):
        @pl.when(jnp.logical_not(has_up))
        def _(k=k):
            field[k, pl.ds(0, width)] = jnp.zeros((width, channels), field.dtype)

        @pl.when(jnp.logical_not(has_down))
        def _(k=k):
            field[k, pl.ds(width + size, width)] = jnp.zeros((width, channels), field.dtype)

    load_act.wait()
    load_held.wait()
    field[U, inner] = (act[...].astype(jnp.float32) + dec * held[...].astype(jnp.float32)).astype(field.dtype)
    load_grad.wait()

    @pl.when(not_last)
    def _():
        top = grad[...].astype(jnp.float32) + (1.0 - dec) * held[...].astype(jnp.float32)
        field[GTOP, inner] = top.astype(field.dtype)

    load_saved.wait()
    pl.semaphore_wait(barrier, count)

    def halo_up(k):
        return pltpu.make_async_remote_copy(
            src_ref=field.at[k, pl.ds(width, width)],
            dst_ref=field.at[k, pl.ds(width + size, width)],
            send_sem=halo_send.at[k, 0],
            recv_sem=halo_recv.at[k, 0],
            device_id=at_up,
            device_id_type=MESH,
        )

    def halo_down(k):
        return pltpu.make_async_remote_copy(
            src_ref=field.at[k, pl.ds(size, width)],
            dst_ref=field.at[k, pl.ds(0, width)],
            send_sem=halo_send.at[k, 1],
            recv_sem=halo_recv.at[k, 1],
            device_id=at_down,
            device_id_type=MESH,
        )

    def send_halo(k):
        @pl.when(has_up)
        def _():
            halo_up(k).start()

        @pl.when(has_down)
        def _():
            halo_down(k).start()

    def wait_halo(k):
        @pl.when(has_up)
        def _():
            halo_up(k).wait_send()
            halo_down(k).wait_recv()

        @pl.when(has_down)
        def _():
            halo_down(k).wait_send()
            halo_up(k).wait_recv()

    send_halo(U)

    @pl.when(not_last)
    def _():
        send_halo(KEPT)
        send_halo(GTOP)

    out_refs = (fwd_out, grad_out, mirror_out)

    def zero_fill(kind):
        return pltpu.make_async_copy(zeros, out_refs[kind], local_sem.at[0])

    @pl.when(jnp.logical_not(has_prev))
    def _():
        zeros[...] = jnp.zeros_like(zeros)
        zero_fill(FWD).start()

    @pl.when(is_last)
    def _():
        zeros[...] = jnp.zeros_like(zeros)
        zero_fill(GRAD).start()

    def columns(n):
        return pl.ds(pl.multiple_of(n * part, part), part)

    def deliver(src, kind, n, where):
        return pltpu.make_async_remote_copy(
            src_ref=src.at[:, columns(n)],
            dst_ref=out_refs[kind].at[:, columns(n)],
            send_sem=out_send.at[kind, n],
            recv_sem=out_recv.at[kind, n],
            device_id=where,
            device_id_type=MESH,
        )

    def conv(k, w, flip, n):
        column = lax.broadcasted_iota(jnp.int32, (size, 1), 0) % width
        total = None
        for b in (0, 2, 1):
            partial = None
            for a in range(3):
                x = field[k, pl.ds(a * width, size)]
                if flip:
                    taps = w[3 * (2 - a) + 2 - b, columns(n), :]
                    dims = (((1,), (1,)), ((), ()))
                else:
                    taps = w[3 * a + b, :, columns(n)]
                    dims = (((1,), (0,)), ((), ()))
                term = lax.dot_general(x, taps, dims, preferred_element_type=jnp.float32)
                partial = term if partial is None else partial + term
            if b == 0:
                partial = jnp.where(column == 0, 0.0, pltpu.roll(partial, 1, 0))
            if b == 2:
                partial = jnp.where(column == width - 1, 0.0, pltpu.roll(partial, size - 1, 0))
            total = partial if total is None else total + partial
        return total

    def step_hidden():
        wait_halo(U)

        def body(n, _):
            value = conv(U, w1, False, n)
            sig = jax.nn.sigmoid(value)
            field[HID, inner, columns(n)] = (value * sig).astype(field.dtype)

            @pl.when(is_last)
            def _():
                slope[:, columns(n)] = sig * (1.0 + value * (1.0 - sig))
            return 0

        lax.fori_loop(0, halves, body, 0)
        send_halo(HID)

    def step_pre():
        wait_halo(KEPT)

        def body(n, _):
            value = conv(KEPT, w1, False, n)
            sig = jax.nn.sigmoid(value)
            slope[:, columns(n)] = sig * (1.0 + value * (1.0 - sig))
            return 0

        lax.fori_loop(0, halves, body, 0)

    def step_output():
        wait_halo(HID)

        def body(n, _):
            base = act[:, columns(n)].astype(jnp.float32) + dec * held[:, columns(n)].astype(jnp.float32)
            value = (base + conv(HID, w2, False, n)).astype(y.dtype)
            y[:, columns(n)] = value

            @pl.when(is_last)
            def _():
                top = value.astype(jnp.float32) - target[:, columns(n)].astype(jnp.float32)
                field[GTOP, inner, columns(n)] = top.astype(field.dtype)

            @pl.when(jnp.logical_and(encoder, jnp.logical_not(middle)))
            def _():
                deliver(y, MIRROR, n, at_mirror).start()

            @pl.when(has_next)
            def _():
                deliver(y, FWD, n, at_next).start()
            return 0

        lax.fori_loop(0, halves, body, 0)

        @pl.when(is_last)
        def _():
            send_halo(GTOP)

    def step_back():
        wait_halo(GTOP)

        def body(n, _):
            value = conv(GTOP, w2, True, n)
            field[GMID, inner, columns(n)] = (slope[:, columns(n)] * value).astype(field.dtype)
            return 0

        lax.fori_loop(0, halves, body, 0)
        send_halo(GMID)

    def step_low():
        wait_halo(GMID)

        def body(n, _):
            base = field[GTOP, inner, columns(n)].astype(jnp.float32)
            low[:, columns(n)] = (base + conv(GMID, w1, True, n)).astype(low.dtype)

            @pl.when(jnp.logical_and(decoder, jnp.logical_not(middle)))
            def _():
                deliver(low, MIRROR, n, at_mirror).start()

            @pl.when(has_prev)
            def _():
                deliver(low, GRAD, n, at_prev).start()
            return 0

        lax.fori_loop(0, halves, body, 0)

    load_w1.wait()
    pl.when(others)(step_hidden)
    pl.when(not_last)(step_pre)
    load_w2.wait()
    load_target.wait()
    pl.when(others)(step_output)
    step_back()
    pl.when(inner_dec)(step_hidden)
    step_low()
    pl.when(inner_dec)(step_output)

    def twin(kind):
        return pltpu.make_async_copy(out_refs[kind], mirror_out, local_sem.at[1])

    @pl.when(has_prev)
    def _():
        for n in range(halves):
            deliver(y, FWD, n, at_next).wait_recv()

    @pl.when(middle_dec)
    def _():
        twin(FWD).start()

    @pl.when(has_next)
    def _():
        for n in range(halves):
            deliver(low, GRAD, n, at_prev).wait_recv()

    @pl.when(middle_enc)
    def _():
        twin(GRAD).start()

    @pl.when(jnp.logical_not(middle))
    def _():
        for n in range(halves):
            deliver(y, MIRROR, n, at_mirror).wait_recv()
            deliver(y, MIRROR, n, at_mirror).wait_send()

    @pl.when(has_next)
    def _():
        for n in range(halves):
            deliver(y, FWD, n, at_next).wait_send()

    @pl.when(has_prev)
    def _():
        for n in range(halves):
            deliver(low, GRAD, n, at_prev).wait_send()

    @pl.when(jnp.logical_not(has_prev))
    def _():
        zero_fill(FWD).wait()

    @pl.when(is_last)
    def _():
        zero_fill(GRAD).wait()

    @pl.when(middle)
    def _():
        twin(FWD).wait()


def on_device(fwd_in, grad_in, saved_in, mirror_held, target, w_first, w_second):
    _, rows, width, channels = fwd_in.shape
    size = rows * width
    taps = w_first.shape[1] * w_first.shape[2]
    halves = 2
    dtype = fwd_in.dtype
    sections = lax.axis_size("section")
    row_devices = lax.axis_size("rows")
    flat = lambda value: value.reshape(size, channels)
    flat_w = lambda value: value.reshape(taps, channels, channels)
    any_spec = pl.BlockSpec(memory_space=pl.ANY)
    plane = pltpu.VMEM((size, channels), dtype)
    weight = pltpu.VMEM((taps, channels, channels), dtype)
    outs = pl.pallas_call(
        functools.partial(relay_kernel, sections, row_devices, width, halves),
        out_shape=[jax.ShapeDtypeStruct((size, channels), dtype)] * 3,
        in_specs=[any_spec] * 7,
        out_specs=[any_spec] * 3,
        scratch_shapes=[
            plane, plane, plane, plane,
            weight, weight,
            pltpu.VMEM((5, size + 2 * width, channels), dtype),
            pltpu.VMEM((size, channels), jnp.float32),
            plane, plane, plane,
            pltpu.SemaphoreType.DMA((7,)),
            pltpu.SemaphoreType.DMA((5, 2)),
            pltpu.SemaphoreType.DMA((5, 2)),
            pltpu.SemaphoreType.DMA((3, halves)),
            pltpu.SemaphoreType.DMA((3, halves)),
            pltpu.SemaphoreType.DMA((2,)),
        ],
        compiler_params=pltpu.CompilerParams(
            collective_id=0, has_side_effects=True, vmem_limit_bytes=48 * 2**20
        ),
        cost_estimate=pl.CostEstimate(
            flops=10 * size * taps * channels * channels,
            bytes_accessed=4 * taps * channels * channels + 16 * size * channels,
            transcendentals=2 * size * channels,
        ),
    )(
        flat(fwd_in), flat(grad_in), flat(saved_in), flat(mirror_held), flat(target),
        flat_w(w_first), flat_w(w_second),
    )
    return tuple(value.reshape(fwd_in.shape) for value in outs)


def solution(mesh):
    blocks = P("section", "rows", None, None)
    weights = P("section", None, None, None, None)
    return jax.shard_map(
        on_device,
        mesh=mesh,
        in_specs=(blocks, blocks, blocks, blocks, P("rows", None, None), weights, weights),
        out_specs=(blocks, blocks, blocks),
        check_vma=False,
    )
```

time: 79.9 us -> 40.8 us (0.51)
  Pallas kernels: 0 us -> 32.2 us
  starting transfers between devices: 22.6 us -> 0 us
  waiting for transfers between devices: 22 us -> 0 us
  matrix products: 18.2 us -> 0 us
  other arithmetic: 6.52 us -> 0 us
  local copies, waits for them, and re-layouts: 9.28 us -> 7.58 us
    pallas_call x0 -> x1, Pallas kernels: none -> 32.2 us  [on_device(): pl.pallas_call(functools.partial(relay_kernel, sections, row_devices, wid...]
    conv_general_dilated x5 -> x0, matrix products: 18.2 us -> none  [conv_rows(): lax.conv_general_dilated(field, kernel, (1, 1), ((0, 0), (1, 1)), dimensi...]
    ppermute x6 -> x0, starting transfers between devices: 15.7 us -> none  [the longest x2 9.21 us: extended(): before = lax.ppermute(last, axis, up)]
    all_to_all x2 -> x0, waiting for transfers between devices: 11.7 us -> none  [the longest x1 6.62 us: on_device(): lax.all_to_all(spread[::-1], 'section', split_axis=0, concat_axis=2, tile...]
    ppermute x6 -> x0, waiting for transfers between devices: 10.2 us -> none  [the longest x2 7.27 us: extended(): after = lax.ppermute(leading, axis, down)]
    all_to_all x2 -> x0, starting transfers between devices: 6.94 us -> none  [the longest x1 3.47 us: on_device(): lax.all_to_all(payload[None], 'section', split_axis=2, concat_axis=0, til...]
    unnamed x18 -> x13, local copies, waits for them, and re-layouts: 4.38 us -> 7.58 us
    conv_general_dilated x8 -> x0, local copies, waits for them, and re-layouts: 2.49 us -> none  [conv_rows(): lax.conv_general_dilated(field, kernel, (1, 1), ((0, 0), (1, 1)), dimensi...]
  transfers between devices with their start and end apart: 8 -> 0, of which waited for: 6 -> 0; matrix products, arithmetic and copies ran while one was open for 4% -> 0% of each run, Pallas kernels for 0% -> 0%
where the time goes in v1:
time: 40.8 us; the launch traced here: 40.5 us
  Pallas kernels  32.2 us (79%)
  local copies, waits for them, and re-layouts  7.58 us (19%)
  between operations  0.65 us (2%)
    pallas_call x1, Pallas kernels, on_device(): pl.pallas_call(functools.partial(relay_kernel, sections, row_devices, wid...  32.2 us
    unnamed x13, local copies, waits for them, and re-layouts  7.58 us

profile of v1, /device:TPU:0, one launch (start us, length us, event | category | flops | bytes accessed | tf_op | source)
XLA Modules:
  0.0 40.5 jit_solution(10356721763811176635)
XLA Ops:
  0.6 0.0 copy-start
  0.6 1.0 %copy-done = bf16[1,16,32,512]{3,2,1,0:T(8,128)(2,1)S(1)} copy-done((bf16[1,16,32,512]{3,2,1,0:T(8,128)(2,1)S(1)}, bf16[1,16,32,512]{3,2,1,0:T(8,128)(2,1)}, u32[]{:S(2)}) %copy-start) | copy-done | bytes 524312
  1.7 0.0 copy-start.1
  1.7 1.0 %copy-done.1 = bf16[1,16,32,512]{3,2,1,0:T(8,128)(2,1)S(1)} copy-done((bf16[1,16,32,512]{3,2,1,0:T(8,128)(2,1)S(1)}, bf16[1,16,32,512]{3,2,1,0:T(8,128)(2,1)}, u32[]{:S(2)}) %copy-start.1) | copy-done | bytes 524312
  2.7 0.0 copy-start.2
  2.7 1.0 %copy-done.2 = bf16[1,16,32,512]{3,2,1,0:T(8,128)(2,1)S(1)} copy-done((bf16[1,16,32,512]{3,2,1,0:T(8,128)(2,1)S(1)}, bf16[1,16,32,512]{3,2,1,0:T(8,128)(2,1)}, u32[]{:S(2)}) %copy-start.2) | copy-done | bytes 524312
  3.8 0.0 copy-start.3
  3.8 1.0 %copy-done.3 = bf16[1,16,32,512]{3,2,1,0:T(8,128)(2,1)S(1)} copy-done((bf16[1,16,32,512]{3,2,1,0:T(8,128)(2,1)S(1)}, bf16[1,16,32,512]{3,2,1,0:T(8,128)(2,1)}, u32[]{:S(2)}) %copy-start.3) | copy-done | bytes 524312
  4.8 0.0 copy-start.4
  4.8 1.0 %copy-done.4 = bf16[16,32,512]{2,1,0:T(8,128)(2,1)S(1)} copy-done((bf16[16,32,512]{2,1,0:T(8,128)(2,1)S(1)}, bf16[16,32,512]{2,1,0:T(8,128)(2,1)}, u32[]{:S(2)}) %copy-start.4) | copy-done | bytes 524312
  5.8 32.2 %shard_map.94 = (bf16[512,512]{1,0:T(8,128)(2,1)S(1)}, bf16[512,512]{1,0:T(8,128)(2,1)S(1)}, bf16[512,512]{1,0:T(8,128)(2,1)S(1)}) custom-call(bf16[512,512]{1,0:T(8,128)(2,1)S(1)} %bitcast.13, bf16[512,512]{1,0:T(8,128)(2,1)S(1)} %bitcast.14, bf16[512,512]{1,0:T(8,128)(2,1)S(1)} %bitcast.15, bf16[512,512]{1,0:T(8,128)(2,1)S(1)} %bitcast.16, ...), custom_call_target="tpu_custom_call" | custom-call | flops 12079595520 | bytes 13631488 | tf_op jit(solution)/shard_map/pallas_call | solution.py:348
  38.1 0.8 %copy.13 = bf16[1,16,32,512]{3,2,1,0:T(8,128)(2,1)} copy(bf16[1,16,32,512]{3,2,1,0:T(8,128)(2,1)S(1)} %bitcast.12) | data formatting | bytes 1048576
  38.9 0.8 %copy.14 = bf16[1,16,32,512]{3,2,1,0:T(8,128)(2,1)} copy(bf16[1,16,32,512]{3,2,1,0:T(8,128)(2,1)S(1)} %bitcast.11) | data formatting | bytes 1048576
  39.7 0.8 %copy.15 = bf16[1,16,32,512]{3,2,1,0:T(8,128)(2,1)} copy(bf16[1,16,32,512]{3,2,1,0:T(8,128)(2,1)S(1)} %bitcast.10) | data formatting | bytes 1048576
Async XLA Ops:
  0.6 1.0 %copy-start = (bf16[1,16,32,512]{3,2,1,0:T(8,128)(2,1)S(1)}, bf16[1,16,32,512]{3,2,1,0:T(8,128)(2,1)}, u32[]{:S(2)}) copy-start(bf16[1,16,32,512]{3,2,1,0:T(8,128)(2,1)} %param.7) | copy-start | bytes 1572868
  1.7 1.0 %copy-start.1 = (bf16[1,16,32,512]{3,2,1,0:T(8,128)(2,1)S(1)}, bf16[1,16,32,512]{3,2,1,0:T(8,128)(2,1)}, u32[]{:S(2)}) copy-start(bf16[1,16,32,512]{3,2,1,0:T(8,128)(2,1)} %param.8) | copy-start | bytes 1572868
  2.7 1.0 %copy-start.2 = (bf16[1,16,32,512]{3,2,1,0:T(8,128)(2,1)S(1)}, bf16[1,16,32,512]{3,2,1,0:T(8,128)(2,1)}, u32[]{:S(2)}) copy-start(bf16[1,16,32,512]{3,2,1,0:T(8,128)(2,1)} %param.9) | copy-start | bytes 1572868
  3.8 1.0 %copy-start.3 = (bf16[1,16,32,512]{3,2,1,0:T(8,128)(2,1)S(1)}, bf16[1,16,32,512]{3,2,1,0:T(8,128)(2,1)}, u32[]{:S(2)}) copy-start(bf16[1,16,32,512]{3,2,1,0:T(8,128)(2,1)} %param.10) | copy-start | bytes 1572868
  4.8 1.0 %copy-start.4 = (bf16[16,32,512]{2,1,0:T(8,128)(2,1)S(1)}, bf16[16,32,512]{2,1,0:T(8,128)(2,1)}, u32[]{:S(2)}) copy-start(bf16[16,32,512]{2,1,0:T(8,128)(2,1)} %param.11) | copy-start | bytes 1572868

commit v2 on v1

v2 whole, which is shorter than its diff:
```python
import functools

import jax
import jax.numpy as jnp
from jax import lax
from jax.experimental import pallas as pl
from jax.experimental.pallas import tpu as pltpu
from jax.sharding import PartitionSpec as P

MESH = pl.DeviceIdType.MESH
U, KEPT, GTOP, HID, GMID = range(5)
FWD, GRAD, MIRROR = range(3)
HALVES = 2


def relay_kernel(
    sections, row_devices, width, chunks,
    act_hbm, grad_hbm, saved_hbm, held_hbm, target_hbm, w1_hbm, w2_hbm,
    fwd_out, grad_out, mirror_out,
    act, grad, held, target, w1, w2, field, slope, y, low,
    in_sem, w_sem, halo_send, halo_recv, out_send, out_recv,
):
    size, channels = act.shape
    part = channels // HALVES
    section = lax.axis_index("section")
    row = lax.axis_index("rows")
    half_sections = sections // 2
    decoder = section >= half_sections
    is_last = section == sections - 1
    dec = decoder.astype(jnp.float32)
    has_up, has_down = row > 0, row < row_devices - 1
    has_prev, has_next = section > 0, section < sections - 1
    mirror = sections - 1 - section
    middle_enc = section == half_sections - 1
    middle_dec = section == half_sections
    middle = jnp.logical_or(middle_enc, middle_dec)
    encoder = jnp.logical_not(decoder)
    inner_dec = jnp.logical_and(decoder, jnp.logical_not(is_last))
    others = jnp.logical_not(inner_dec)
    not_last = jnp.logical_not(is_last)
    at_up = (section, row - 1)
    at_down = (section, row + 1)
    at_prev = (section - 1, row)
    at_next = (section + 1, row)
    at_mirror = (mirror, row)

    inner = pl.ds(width, size)

    def load(src, dst, k):
        return pltpu.make_async_copy(src, dst, in_sem.at[k])

    load_act = load(act_hbm, act, 0)
    load_held = load(held_hbm, held, 1)
    load_grad = load(grad_hbm, grad, 2)
    load_saved = load(saved_hbm, field.at[KEPT, inner], 3)
    load_target = load(target_hbm, target, 4)

    def load_tap(j, a, b):
        t = 3 * a + b
        src, dst = ((w1_hbm, w1), (w2_hbm, w2))[j]
        return pltpu.make_async_copy(src.at[t], dst.at[t], w_sem.at[j, t])

    taps = [(a, b) for a in (1, 0, 2) for b in (0, 2, 1)]
    for copy in (load_act, load_held, load_saved):
        copy.start()
    for a, b in taps:
        load_tap(0, a, b).start()
    for copy in (load_grad, load_target):
        copy.start()

    barrier = pltpu.get_barrier_semaphore()
    partners = ((has_up, at_up), (has_down, at_down), (has_prev, at_prev), (has_next, at_next))
    count = jnp.int32(1)
    for cond, where in partners:
        @pl.when(cond)
        def _(where=where):
            pl.semaphore_signal(barrier, inc=1, device_id=where, device_id_type=MESH)
        count = count + cond.astype(jnp.int32)
    pl.semaphore_signal(barrier, inc=1, device_id=at_mirror, device_id_type=MESH)

    for k in range(5):
        @pl.when(jnp.logical_not(has_up))
        def _(k=k):
            field[k, pl.ds(0, width)] = jnp.zeros((width, channels), field.dtype)

        @pl.when(jnp.logical_not(has_down))
        def _(k=k):
            field[k, pl.ds(width + size, width)] = jnp.zeros((width, channels), field.dtype)

    def columns(n):
        return pl.ds(n * part, part)

    def halo_up(k, n):
        return pltpu.make_async_remote_copy(
            src_ref=field.at[k, pl.ds(width, width), columns(n)],
            dst_ref=field.at[k, pl.ds(width + size, width), columns(n)],
            send_sem=halo_send.at[k, 0, n],
            recv_sem=halo_recv.at[k, 0, n],
            device_id=at_up,
            device_id_type=MESH,
        )

    def halo_down(k, n):
        return pltpu.make_async_remote_copy(
            src_ref=field.at[k, pl.ds(size, width), columns(n)],
            dst_ref=field.at[k, pl.ds(0, width), columns(n)],
            send_sem=halo_send.at[k, 1, n],
            recv_sem=halo_recv.at[k, 1, n],
            device_id=at_down,
            device_id_type=MESH,
        )

    def send_halo(k, n):
        @pl.when(has_up)
        def _():
            halo_up(k, n).start()

        @pl.when(has_down)
        def _():
            halo_down(k, n).start()

    def wait_halo(k):
        @pl.when(has_up)
        def _():
            for n in range(HALVES):
                halo_up(k, n).wait_send()
                halo_down(k, n).wait_recv()

        @pl.when(has_down)
        def _():
            for n in range(HALVES):
                halo_down(k, n).wait_send()
                halo_up(k, n).wait_recv()

    load_act.wait()
    load_held.wait()
    field[U, inner] = (act[...].astype(jnp.float32) + dec * held[...].astype(jnp.float32)).astype(field.dtype)
    pl.semaphore_wait(barrier, count)
    for n in range(HALVES):
        send_halo(U, n)
    load_saved.wait()
    load_grad.wait()

    @pl.when(not_last)
    def _():
        for n in range(HALVES):
            send_halo(KEPT, n)
        top = grad[...].astype(jnp.float32) + (1.0 - dec) * held[...].astype(jnp.float32)
        field[GTOP, inner] = top.astype(field.dtype)
        for n in range(HALVES):
            send_halo(GTOP, n)

    for a, b in taps:
        load_tap(1, a, b).start()

    out_refs = (fwd_out, grad_out, mirror_out)

    def deliver(src, kind, c, where):
        n, first, count = chunks[c]
        at = (pl.ds(first, count), columns(n))
        return pltpu.make_async_remote_copy(
            src_ref=src.at[at],
            dst_ref=out_refs[kind].at[at],
            send_sem=out_send.at[kind, c],
            recv_sem=out_recv.at[kind, c],
            device_id=where,
            device_id_type=MESH,
        )

    def conv(k, w, flip, n, first=0, count=size, fresh=False, arrive=None):
        column = lax.broadcasted_iota(jnp.int32, (count, 1), 0) % width
        total = None
        for group in ((1,), (0, 2)) if fresh else ((1, 0, 2),):
            if fresh and 0 in group:
                wait_halo(k)
            for b in (0, 2, 1):
                partial = None
                for a in group:
                    if arrive is not None:
                        arrive(a, b)
                    x = field[k, pl.ds(first + a * width, count)]
                    if flip:
                        tap = w[3 * (2 - a) + 2 - b, columns(n), :]
                        dims = (((1,), (1,)), ((), ()))
                    else:
                        tap = w[3 * a + b, :, columns(n)]
                        dims = (((1,), (0,)), ((), ()))
                    term = lax.dot_general(x, tap, dims, preferred_element_type=jnp.float32)
                    partial = term if partial is None else partial + term
                if b == 0:
                    partial = jnp.where(column == 0, 0.0, pltpu.roll(partial, 1, 0))
                if b == 2:
                    partial = jnp.where(column == width - 1, 0.0, pltpu.roll(partial, count - 1, 0))
                total = partial if total is None else total + partial
        return total

    def first_tap(a, b):
        load_tap(0, a, b).wait()

    def step_hidden(arrive=None):
        for n in range(HALVES):
            value = conv(U, w1, False, n, fresh=n == 0, arrive=arrive if n == 0 else None)
            sig = jax.nn.sigmoid(value)
            field[HID, inner, columns(n)] = (value * sig).astype(field.dtype)
            send_halo(HID, n)

            @pl.when(is_last)
            def _():
                slope[:, columns(n)] = sig * (1.0 + value * (1.0 - sig))

    def step_pre(arrive=None):
        for n in range(HALVES):
            value = conv(KEPT, w1, False, n, fresh=n == 0, arrive=arrive if n == 0 else None)
            sig = jax.nn.sigmoid(value)
            slope[:, columns(n)] = sig * (1.0 + value * (1.0 - sig))

    def step_output():
        for c, (n, first, count) in enumerate(chunks):
            at = (pl.ds(first, count), columns(n))
            base = act[at].astype(jnp.float32) + dec * held[at].astype(jnp.float32)
            value = (base + conv(HID, w2, False, n, first, count, fresh=c == 0)).astype(y.dtype)
            y[at] = value

            @pl.when(is_last)
            def _():
                top = value.astype(jnp.float32) - target[at].astype(jnp.float32)
                field[GTOP, pl.ds(width + first, count), columns(n)] = top.astype(field.dtype)
                if first + count == size:
                    send_halo(GTOP, n)

            @pl.when(jnp.logical_and(encoder, jnp.logical_not(middle)))
            def _():
                deliver(y, MIRROR, c, at_mirror).start()

            @pl.when(has_next)
            def _():
                deliver(y, FWD, c, at_next).start()

    def step_back():
        for n in range(HALVES):
            value = conv(GTOP, w2, True, n, fresh=n == 0)
            field[GMID, inner, columns(n)] = (slope[:, columns(n)] * value).astype(field.dtype)
            send_halo(GMID, n)

    def step_low():
        for c, (n, first, count) in enumerate(chunks):
            at = (pl.ds(first, count), columns(n))
            base = field[GTOP, pl.ds(width + first, count), columns(n)].astype(jnp.float32)
            low[at] = (base + conv(GMID, w1, True, n, first, count, fresh=c == 0)).astype(low.dtype)

            @pl.when(jnp.logical_and(decoder, jnp.logical_not(middle)))
            def _():
                deliver(low, MIRROR, c, at_mirror).start()

            @pl.when(has_prev)
            def _():
                deliver(low, GRAD, c, at_prev).start()

    pl.when(others)(lambda: step_hidden(first_tap))
    pl.when(inner_dec)(lambda: step_pre(first_tap))
    pl.when(encoder)(step_pre)
    load_target.wait()
    for a, b in taps:
        load_tap(1, a, b).wait()
    pl.when(others)(step_output)
    step_back()
    step_low()
    pl.when(inner_dec)(step_hidden)
    pl.when(inner_dec)(step_output)

    def drain(cond, src, kind, where, sent):
        @pl.when(cond)
        def _():
            for c in range(len(chunks)):
                copy = deliver(src, kind, c, where)
                (copy.wait_send if sent else copy.wait_recv)()

    apart = jnp.logical_not(middle)
    drain(has_prev, y, FWD, at_next, False)
    drain(has_next, low, GRAD, at_prev, False)
    drain(apart, y, MIRROR, at_mirror, False)
    drain(has_next, y, FWD, at_next, True)
    drain(has_prev, low, GRAD, at_prev, True)
    drain(apart, y, MIRROR, at_mirror, True)


def finish_kernel(sections, pieces, fwd, grad, mirror, fwd_out, grad_out, mirror_out, zeros, sem):
    section = lax.axis_index("section")
    size = zeros.shape[0]
    piece = size // pieces
    is_first, is_last = section == 0, section == sections - 1
    middle_enc = section == sections // 2 - 1
    middle_dec = section == sections // 2
    apart = jnp.logical_not(jnp.logical_or(middle_enc, middle_dec))
    moves = (
        (jnp.logical_not(is_first), fwd, fwd_out, 0),
        (is_first, zeros, fwd_out, 0),
        (jnp.logical_not(is_last), grad, grad_out, 1),
        (is_last, zeros, grad_out, 1),
        (middle_dec, fwd, mirror_out, 2),
        (middle_enc, grad, mirror_out, 2),
        (apart, mirror, mirror_out, 2),
    )

    def copies(src, dst, k):
        for p in range(pieces):
            rows = pl.ds(p * piece, piece)
            yield pltpu.make_async_copy(src.at[rows], dst.at[rows], sem.at[k, p])

    @pl.when(jnp.logical_or(is_first, is_last))
    def _():
        zeros[...] = jnp.zeros_like(zeros)

    for cond, src, dst, k in moves:
        @pl.when(cond)
        def _(src=src, dst=dst, k=k):
            for copy in copies(src, dst, k):
                copy.start()
    for dst, k in ((fwd_out, 0), (grad_out, 1), (mirror_out, 2)):
        for copy in copies(zeros, dst, k):
            copy.wait()


def on_device(fwd_in, grad_in, saved_in, mirror_held, target, w_first, w_second):
    _, rows, width, channels = fwd_in.shape
    size = rows * width
    taps = w_first.shape[1] * w_first.shape[2]
    chunks = ((0, 0, size), (1, 0, size // 2), (1, size // 2, size // 2))
    dtype = fwd_in.dtype
    sections = lax.axis_size("section")
    row_devices = lax.axis_size("rows")
    flat = lambda value: value.reshape(size, channels)
    flat_w = lambda value: value.reshape(taps, channels, channels)
    any_spec = pl.BlockSpec(memory_space=pl.ANY)
    hbm_spec = pl.BlockSpec(memory_space=pltpu.HBM)
    plane = pltpu.VMEM((size, channels), dtype)
    weight = pltpu.VMEM((taps, channels, channels), dtype)
    outs = pl.pallas_call(
        functools.partial(relay_kernel, sections, row_devices, width, chunks),
        out_shape=[jax.ShapeDtypeStruct((size, channels), dtype)] * 3,
        in_specs=[hbm_spec] * 7,
        out_specs=[any_spec] * 3,
        scratch_shapes=[
            plane, plane, plane, plane,
            weight, weight,
            pltpu.VMEM((5, size + 2 * width, channels), dtype),
            pltpu.VMEM((size, channels), jnp.float32),
            plane, plane,
            pltpu.SemaphoreType.DMA((5,)),
            pltpu.SemaphoreType.DMA((2, taps)),
            pltpu.SemaphoreType.DMA((5, 2, HALVES)),
            pltpu.SemaphoreType.DMA((5, 2, HALVES)),
            pltpu.SemaphoreType.DMA((3, len(chunks))),
            pltpu.SemaphoreType.DMA((3, len(chunks))),
        ],
        compiler_params=pltpu.CompilerParams(
            collective_id=0, has_side_effects=True, vmem_limit_bytes=62 * 2**20
        ),
        cost_estimate=pl.CostEstimate(
            flops=10 * size * taps * channels * channels,
            bytes_accessed=4 * taps * channels * channels + 16 * size * channels,
            transcendentals=2 * size * channels,
        ),
    )(
        flat(fwd_in), flat(grad_in), flat(saved_in), flat(mirror_held), flat(target),
        flat_w(w_first), flat_w(w_second),
    )
    pieces = 2
    outs = pl.pallas_call(
        functools.partial(finish_kernel, sections, pieces),
        out_shape=[jax.ShapeDtypeStruct((size, channels), dtype)] * 3,
        in_specs=[any_spec] * 3,
        out_specs=[hbm_spec] * 3,
        scratch_shapes=[plane, pltpu.SemaphoreType.DMA((3, pieces))],
        compiler_params=pltpu.CompilerParams(vmem_limit_bytes=62 * 2**20),
    )(*outs)
    return tuple(value.reshape(fwd_in.shape) for value in outs)


def solution(mesh):
    blocks = P("section", "rows", None, None)
    weights = P("section", None, None, None, None)
    return jax.shard_map(
        on_device,
        mesh=mesh,
        in_specs=(blocks, blocks, blocks, blocks, P("rows", None, None), weights, weights),
        out_specs=(blocks, blocks, blocks),
        check_vma=False,
    )
```

time: 40.8 us -> 82.6 us (2.02)
  the two profiles are of different devices: /device:TPU:0 before, /device:TPU:10 now
where the time goes in v2:
time: 82.6 us; the launch traced here: 82.5 us
  Pallas kernels  81.7 us (99%)
    pallas_call x1, Pallas kernels, on_device(): pl.pallas_call(functools.partial(finish_kernel, sections, pieces), out_sh...  48.8 us
    pallas_call x1, Pallas kernels, on_device(): pl.pallas_call(functools.partial(relay_kernel, sections, row_devices, wid...  32.9 us

profile of v2, /device:TPU:10, one launch (start us, length us, event | category | flops | bytes accessed | tf_op | source)
XLA Modules:
  0.0 82.5 jit_solution(7166357099953776611)
XLA Ops:
  0.6 32.9 %shard_map.94 = (bf16[512,512]{1,0:T(8,128)(2,1)}, bf16[512,512]{1,0:T(8,128)(2,1)}, bf16[512,512]{1,0:T(8,128)(2,1)}) custom-call(bf16[512,512]{1,0:T(8,128)(2,1)} %bitcast.12, bf16[512,512]{1,0:T(8,128)(2,1)} %bitcast.13, bf16[512,512]{1,0:T(8,128)(2,1)} %bitcast.14, bf16[512,512]{1,0:T(8,128)(2,1)} %bitcast.15, bf16[512,512]{1,0:T(8,128)(2,1)} %bitcast.16, ...), custom_call_target="tpu_custom_call" | custom-call | flops 12079595520 | bytes 13631488 | tf_op jit(solution)/shard_map/pallas_call | solution.py:338
  33.5 48.8 %shard_map.95 = (bf16[512,512]{1,0:T(8,128)(2,1)}, bf16[512,512]{1,0:T(8,128)(2,1)}, bf16[512,512]{1,0:T(8,128)(2,1)}) custom-call(bf16[512,512]{1,0:T(8,128)(2,1)} %get-tuple-element.9.fwd, bf16[512,512]{1,0:T(8,128)(2,1)} %get-tuple-element.10.grad, bf16[512,512]{1,0:T(8,128)(2,1)} %get-tuple-element.11.mirror), custom_call_target="tpu_custom_call" | custom-call | tf_op jit(solution)/shard_map/pallas_call | solution.py:369

commit v3 on v2

--- a/solution.py
+++ b/solution.py
@@ -60,7 +60,7 @@
         src, dst = ((w1_hbm, w1), (w2_hbm, w2))[j]
         return pltpu.make_async_copy(src.at[t], dst.at[t], w_sem.at[j, t])
 
-    taps = [(a, b) for a in (1, 0, 2) for b in (0, 2, 1)]
+    taps = [(a, b) for a in (1, 2, 0) for b in range(3)]
     for copy in (load_act, load_held, load_saved):
         copy.start()
     for a, b in taps:
@@ -167,64 +167,102 @@
             device_id_type=MESH,
         )
 
-    def conv(k, w, flip, n, first=0, count=size, fresh=False, arrive=None):
-        column = lax.broadcasted_iota(jnp.int32, (count, 1), 0) % width
-        total = None
-        for group in ((1,), (0, 2)) if fresh else ((1, 0, 2),):
+    def product(k, w, flip, b, group, n, first, count):
+        x = [field[k, pl.ds(first + a * width, count)] for a in group]
+        if flip:
+            tap = [w[3 * (2 - a) + 2 - b, columns(n), :] for a in group]
+            dims = (((1,), (1,)), ((), ()))
+        else:
+            tap = [w[3 * a + b, :, columns(n)] for a in group]
+            dims = (((1,), (0,)), ((), ()))
+        if len(group) > 1:
+            x, tap = jnp.concatenate(x, 1), jnp.concatenate(tap, 1 if flip else 0)
+        else:
+            x, tap = x[0], tap[0]
+        return lax.dot_general(x, tap, dims, preferred_element_type=jnp.float32)
+
+    def partials(k, w, flip, n, first, count, fresh=False, arrive=None):
+        groups = ((1, 2), (0,)) if fresh else ((0, 1, 2),)
+        out = None
+        for group in groups:
             if fresh and 0 in group:
                 wait_halo(k)
-            for b in (0, 2, 1):
-                partial = None
-                for a in group:
-                    if arrive is not None:
+            if arrive is not None:
+                for b in range(3):
+                    for a in group:
                         arrive(a, b)
-                    x = field[k, pl.ds(first + a * width, count)]
-                    if flip:
-                        tap = w[3 * (2 - a) + 2 - b, columns(n), :]
-                        dims = (((1,), (1,)), ((), ()))
-                    else:
-                        tap = w[3 * a + b, :, columns(n)]
-                        dims = (((1,), (0,)), ((), ()))
-                    term = lax.dot_general(x, tap, dims, preferred_element_type=jnp.float32)
-                    partial = term if partial is None else partial + term
-                if b == 0:
-                    partial = jnp.where(column == 0, 0.0, pltpu.roll(partial, 1, 0))
-                if b == 2:
-                    partial = jnp.where(column == width - 1, 0.0, pltpu.roll(partial, count - 1, 0))
-                total = partial if total is None else total + partial
-        return total
+            terms = [product(k, w, flip, b, group, n, first, count) for b in range(3)]
+            out = terms if out is None else [p + q for p, q in zip(out, terms)]
+        return out
+
+    def merged(parts):
+        left, centre, right = parts
+        count = centre.shape[0]
+        column = lax.broadcasted_iota(jnp.int32, (count, 1), 0) % width
+        left = jnp.where(column == 0, 0.0, pltpu.roll(left, 1, 0))
+        right = jnp.where(column == width - 1, 0.0, pltpu.roll(right, count - 1, 0))
+        return left + centre + right
+
+    def run(k, w, flip, store, send=None, arrive=None):
+        waiting = None
+
+        def flush(c, parts):
+            n, first, count = chunks[c]
+            store(n, first, count, merged(parts))
+
+        for c, (n, first, count) in enumerate(chunks):
+            parts = partials(k, w, flip, n, first, count, c == 0, arrive if c == 0 else None)
+            if waiting is not None:
+                flush(*waiting)
+                if send is not None:
+                    send(waiting[0])
+            waiting = (c, parts)
+        flush(*waiting)
+        if send is not None:
+            send(waiting[0])
 
     def first_tap(a, b):
         load_tap(0, a, b).wait()
 
+    def halo_after(k):
+        def send(c):
+            n, first, count = chunks[c]
+            if first + count == size:
+                send_halo(k, n)
+        return send
+
+    def body(first, count):
+        return pl.ds(width + first, count)
+
     def step_hidden(arrive=None):
-        for n in range(HALVES):
-            value = conv(U, w1, False, n, fresh=n == 0, arrive=arrive if n == 0 else None)
+        def store(n, first, count, value):
             sig = jax.nn.sigmoid(value)
-            field[HID, inner, columns(n)] = (value * sig).astype(field.dtype)
-            send_halo(HID, n)
+            field[HID, body(first, count), columns(n)] = (value * sig).astype(field.dtype)
+            slope[pl.ds(first, count), columns(n)] = sig * (1.0 + value * (1.0 - sig))
+
+        run(U, w1, False, store, halo_after(HID), arrive)
+
+    def step_pre(arrive=None):
+        def store(n, first, count, value):
+            sig = jax.nn.sigmoid(value)
+            slope[pl.ds(first, count), columns(n)] = sig * (1.0 + value * (1.0 - sig))
+
+        run(KEPT, w1, False, store, None, arrive)
+
+    def step_output():
+        def store(n, first, count, value):
+            at = (pl.ds(first, count), columns(n))
+            base = act[at].astype(jnp.float32) + dec * held[at].astype(jnp.float32)
+            y[at] = (base + value).astype(y.dtype)
+
+        def send(c):
+            n, first, count = chunks[c]
 
             @pl.when(is_last)
             def _():
-                slope[:, columns(n)] = sig * (1.0 + value * (1.0 - sig))
-
-    def step_pre(arrive=None):
-        for n in range(HALVES):
-            value = conv(KEPT, w1, False, n, fresh=n == 0, arrive=arrive if n == 0 else None)
-            sig = jax.nn.sigmoid(value)
-            slope[:, columns(n)] = sig * (1.0 + value * (1.0 - sig))
-
-    def step_output():
-        for c, (n, first, count) in enumerate(chunks):
-            at = (pl.ds(first, count), columns(n))
-            base = act[at].astype(jnp.float32) + dec * held[at].astype(jnp.float32)
-            value = (base + conv(HID, w2, False, n, first, count, fresh=c == 0)).astype(y.dtype)
-            y[at] = value
-
-            @pl.when(is_last)
-            def _():
-                top = value.astype(jnp.float32) - target[at].astype(jnp.float32)
-                field[GTOP, pl.ds(width + first, count), columns(n)] = top.astype(field.dtype)
+                at = (pl.ds(first, count), columns(n))
+                top = y[at].astype(jnp.float32) - target[at].astype(jnp.float32)
+                field[GTOP, body(first, count), columns(n)] = top.astype(field.dtype)
                 if first + count == size:
                     send_halo(GTOP, n)
 
@@ -236,18 +274,21 @@
             def _():
                 deliver(y, FWD, c, at_next).start()
 
+        run(HID, w2, False, store, send)
+
     def step_back():
-        for n in range(HALVES):
-            value = conv(GTOP, w2, True, n, fresh=n == 0)
-            field[GMID, inner, columns(n)] = (slope[:, columns(n)] * value).astype(field.dtype)
-            send_halo(GMID, n)
+        def store(n, first, count, value):
+            at = (pl.ds(first, count), columns(n))
+            field[GMID, body(first, count), columns(n)] = (slope[at] * value).astype(field.dtype)
+
+        run(GTOP, w2, True, store, halo_after(GMID))
 
     def step_low():
-        for c, (n, first, count) in enumerate(chunks):
-            at = (pl.ds(first, count), columns(n))
-            base = field[GTOP, pl.ds(width + first, count), columns(n)].astype(jnp.float32)
-            low[at] = (base + conv(GMID, w1, True, n, first, count, fresh=c == 0)).astype(low.dtype)
-
+        def store(n, first, count, value):
+            base = field[GTOP, body(first, count), columns(n)].astype(jnp.float32)
+            low[pl.ds(first, count), columns(n)] = (base + value).astype(low.dtype)
+
+        def send(c):
             @pl.when(jnp.logical_and(decoder, jnp.logical_not(middle)))
             def _():
                 deliver(low, MIRROR, c, at_mirror).start()
@@ -255,6 +296,8 @@
             @pl.when(has_prev)
             def _():
                 deliver(low, GRAD, c, at_prev).start()
+
+        run(GMID, w1, True, store, send)
 
     pl.when(others)(lambda: step_hidden(first_tap))
     pl.when(inner_dec)(lambda: step_pre(first_tap))
@@ -325,7 +368,8 @@
     _, rows, width, channels = fwd_in.shape
     size = rows * width
     taps = w_first.shape[1] * w_first.shape[2]
-    chunks = ((0, 0, size), (1, 0, size // 2), (1, size // 2, size // 2))
+    half = size // 2
+    chunks = tuple((n, first, half) for n in range(HALVES) for first in (0, half))
     dtype = fwd_in.dtype
     sections = lax.axis_size("section")
     row_devices = lax.axis_size("rows")
@@ -369,7 +413,7 @@
     outs = pl.pallas_call(
         functools.partial(finish_kernel, sections, pieces),
         out_shape=[jax.ShapeDtypeStruct((size, channels), dtype)] * 3,
-        in_specs=[any_spec] * 3,
+        in_specs=[pl.BlockSpec(memory_space=pltpu.VMEM)] * 3,
         out_specs=[hbm_spec] * 3,
         scratch_shapes=[plane, pltpu.SemaphoreType.DMA((3, pieces))],
         compiler_params=pltpu.CompilerParams(vmem_limit_bytes=62 * 2**20),

time: 82.6 us -> 37.9 us (0.46)
  the two profiles are of different devices: /device:TPU:10 before, /device:TPU:0 now
where the time goes in v3:
time: 37.9 us; the launch traced here: 37.8 us
  Pallas kernels  37 us (98%)
  between operations  0.8 us (2%)
    pallas_call x1, Pallas kernels, on_device(): pl.pallas_call(functools.partial(relay_kernel, sections, row_devices, wid...  34.4 us
    pallas_call x1, Pallas kernels, on_device(): pl.pallas_call(functools.partial(finish_kernel, sections, pieces), out_sh...  2.58 us

profile of v3, /device:TPU:0, one launch (start us, length us, event | category | flops | bytes accessed | tf_op | source)
XLA Modules:
  0.0 37.8 jit_solution(12192377155214231233)
XLA Ops:
  0.6 34.4 %shard_map.94 = (bf16[512,512]{1,0:T(8,128)(2,1)}, bf16[512,512]{1,0:T(8,128)(2,1)}, bf16[512,512]{1,0:T(8,128)(2,1)}) custom-call(bf16[512,512]{1,0:T(8,128)(2,1)} %bitcast.12, bf16[512,512]{1,0:T(8,128)(2,1)} %bitcast.13, bf16[512,512]{1,0:T(8,128)(2,1)} %bitcast.14, bf16[512,512]{1,0:T(8,128)(2,1)} %bitcast.15, bf16[512,512]{1,0:T(8,128)(2,1)} %bitcast.16, ...), custom_call_target="tpu_custom_call" | custom-call | flops 12079595520 | bytes 13631488 | tf_op jit(solution)/shard_map/pallas_call | solution.py:382
  35.1 2.6 %shard_map.95 = (bf16[512,512]{1,0:T(8,128)(2,1)}, bf16[512,512]{1,0:T(8,128)(2,1)}, bf16[512,512]{1,0:T(8,128)(2,1)}) custom-call(bf16[512,512]{1,0:T(8,128)(2,1)} %get-tuple-element.9.fwd, bf16[512,512]{1,0:T(8,128)(2,1)} %get-tuple-element.10.grad, bf16[512,512]{1,0:T(8,128)(2,1)} %get-tuple-element.11.mirror), custom_call_target="tpu_custom_call" | custom-call | tf_op jit(solution)/shard_map/pallas_call | solution.py:413

commit v4 on v2

--- a/solution.py
+++ b/solution.py
@@ -14,11 +14,11 @@
 
 
 def relay_kernel(
-    sections, row_devices, width, chunks,
+    sections, row_devices, width,
     act_hbm, grad_hbm, saved_hbm, held_hbm, target_hbm, w1_hbm, w2_hbm,
     fwd_out, grad_out, mirror_out,
     act, grad, held, target, w1, w2, field, slope, y, low,
-    in_sem, w_sem, halo_send, halo_recv, out_send, out_recv,
+    in_sem, halo_send, halo_recv, out_send, out_recv,
 ):
     size, channels = act.shape
     part = channels // HALVES
@@ -55,17 +55,9 @@
     load_saved = load(saved_hbm, field.at[KEPT, inner], 3)
     load_target = load(target_hbm, target, 4)
 
-    def load_tap(j, a, b):
-        t = 3 * a + b
-        src, dst = ((w1_hbm, w1), (w2_hbm, w2))[j]
-        return pltpu.make_async_copy(src.at[t], dst.at[t], w_sem.at[j, t])
-
-    taps = [(a, b) for a in (1, 0, 2) for b in (0, 2, 1)]
-    for copy in (load_act, load_held, load_saved):
-        copy.start()
-    for a, b in taps:
-        load_tap(0, a, b).start()
-    for copy in (load_grad, load_target):
+    load_w1 = load(w1_hbm, w1, 5)
+    load_w2 = load(w2_hbm, w2, 6)
+    for copy in (load_act, load_held, load_saved, load_w1, load_grad, load_target, load_w2):
         copy.start()
 
     barrier = pltpu.get_barrier_semaphore()
@@ -88,7 +80,7 @@
             field[k, pl.ds(width + size, width)] = jnp.zeros((width, channels), field.dtype)
 
     def columns(n):
-        return pl.ds(n * part, part)
+        return pl.ds(pl.multiple_of(n * part, part), part)
 
     def halo_up(k, n):
         return pltpu.make_async_remote_copy(
@@ -150,14 +142,16 @@
         for n in range(HALVES):
             send_halo(GTOP, n)
 
-    for a, b in taps:
-        load_tap(1, a, b).start()
-
     out_refs = (fwd_out, grad_out, mirror_out)
 
+    tile = size // HALVES
+
+    def place(c, offset=0):
+        n, m = c // HALVES, c % HALVES
+        return (pl.ds(pl.multiple_of(offset + m * tile, width), tile), columns(n))
+
     def deliver(src, kind, c, where):
-        n, first, count = chunks[c]
-        at = (pl.ds(first, count), columns(n))
+        at = place(c)
         return pltpu.make_async_remote_copy(
             src_ref=src.at[at],
             dst_ref=out_refs[kind].at[at],
@@ -167,66 +161,77 @@
             device_id_type=MESH,
         )
 
-    def conv(k, w, flip, n, first=0, count=size, fresh=False, arrive=None):
-        column = lax.broadcasted_iota(jnp.int32, (count, 1), 0) % width
-        total = None
-        for group in ((1,), (0, 2)) if fresh else ((1, 0, 2),):
-            if fresh and 0 in group:
-                wait_halo(k)
-            for b in (0, 2, 1):
-                partial = None
-                for a in group:
-                    if arrive is not None:
-                        arrive(a, b)
-                    x = field[k, pl.ds(first + a * width, count)]
-                    if flip:
-                        tap = w[3 * (2 - a) + 2 - b, columns(n), :]
-                        dims = (((1,), (1,)), ((), ()))
-                    else:
-                        tap = w[3 * a + b, :, columns(n)]
-                        dims = (((1,), (0,)), ((), ()))
-                    term = lax.dot_general(x, tap, dims, preferred_element_type=jnp.float32)
-                    partial = term if partial is None else partial + term
-                if b == 0:
-                    partial = jnp.where(column == 0, 0.0, pltpu.roll(partial, 1, 0))
-                if b == 2:
-                    partial = jnp.where(column == width - 1, 0.0, pltpu.roll(partial, count - 1, 0))
-                total = partial if total is None else total + partial
-        return total
-
-    def first_tap(a, b):
-        load_tap(0, a, b).wait()
-
-    def step_hidden(arrive=None):
-        for n in range(HALVES):
-            value = conv(U, w1, False, n, fresh=n == 0, arrive=arrive if n == 0 else None)
+    def product(k, w, flip, b, c):
+        n, m = c // HALVES, c % HALVES
+        x = [field[k, pl.ds(pl.multiple_of(m * tile + a * width, width), tile)] for a in range(3)]
+        if flip:
+            tap = [w[3 * (2 - a) + 2 - b, columns(n), :] for a in range(3)]
+            dims = (((1,), (1,)), ((), ()))
+        else:
+            tap = [w[3 * a + b, :, columns(n)] for a in range(3)]
+            dims = (((1,), (0,)), ((), ()))
+        x, tap = jnp.concatenate(x, 1), jnp.concatenate(tap, 1 if flip else 0)
+        return lax.dot_general(x, tap, dims, preferred_element_type=jnp.float32)
+
+    def conv(k, w, flip, c):
+        column = lax.broadcasted_iota(jnp.int32, (tile, 1), 0) % width
+        left, centre, right = [product(k, w, flip, b, c) for b in range(3)]
+        left = jnp.where(column == 0, 0.0, pltpu.roll(left, 1, 0))
+        right = jnp.where(column == width - 1, 0.0, pltpu.roll(right, tile - 1, 0))
+        return left + centre + right
+
+    def run(k, body):
+        wait_halo(k)
+
+        def step(c, _):
+            body(c)
+            return 0
+
+        lax.fori_loop(0, HALVES * HALVES, step, 0)
+
+    def send_part(k, c):
+        n, m = c // HALVES, c % HALVES
+
+        @pl.when(jnp.logical_and(has_up, m == 0))
+        def _():
+            halo_up(k, n).start()
+
+        @pl.when(jnp.logical_and(has_down, m == HALVES - 1))
+        def _():
+            halo_down(k, n).start()
+
+    def step_hidden():
+        def body(c):
+            value = conv(U, w1, False, c)
             sig = jax.nn.sigmoid(value)
-            field[HID, inner, columns(n)] = (value * sig).astype(field.dtype)
-            send_halo(HID, n)
+            at = place(c, width)
+            field[HID, at[0], at[1]] = (value * sig).astype(field.dtype)
+            slope[place(c)] = sig * (1.0 + value * (1.0 - sig))
+            send_part(HID, c)
+
+        run(U, body)
+
+    def step_pre():
+        def body(c):
+            value = conv(KEPT, w1, False, c)
+            sig = jax.nn.sigmoid(value)
+            slope[place(c)] = sig * (1.0 + value * (1.0 - sig))
+
+        run(KEPT, body)
+
+    def step_output():
+        def body(c):
+            at = place(c)
+            base = act[at].astype(jnp.float32) + dec * held[at].astype(jnp.float32)
+            value = (base + conv(HID, w2, False, c)).astype(y.dtype)
+            y[at] = value
 
             @pl.when(is_last)
             def _():
-                slope[:, columns(n)] = sig * (1.0 + value * (1.0 - sig))
-
-    def step_pre(arrive=None):
-        for n in range(HALVES):
-            value = conv(KEPT, w1, False, n, fresh=n == 0, arrive=arrive if n == 0 else None)
-            sig = jax.nn.sigmoid(value)
-            slope[:, columns(n)] = sig * (1.0 + value * (1.0 - sig))
-
-    def step_output():
-        for c, (n, first, count) in enumerate(chunks):
-            at = (pl.ds(first, count), columns(n))
-            base = act[at].astype(jnp.float32) + dec * held[at].astype(jnp.float32)
-            value = (base + conv(HID, w2, False, n, first, count, fresh=c == 0)).astype(y.dtype)
-            y[at] = value
-
-            @pl.when(is_last)
-            def _():
                 top = value.astype(jnp.float32) - target[at].astype(jnp.float32)
-                field[GTOP, pl.ds(width + first, count), columns(n)] = top.astype(field.dtype)
-                if first + count == size:
-                    send_halo(GTOP, n)
+                low_at = place(c, width)
+                field[GTOP, low_at[0], low_at[1]] = top.astype(field.dtype)
+                send_part(GTOP, c)
 
             @pl.when(jnp.logical_and(encoder, jnp.logical_not(middle)))
             def _():
@@ -236,17 +241,21 @@
             def _():
                 deliver(y, FWD, c, at_next).start()
 
+        run(HID, body)
+
     def step_back():
-        for n in range(HALVES):
-            value = conv(GTOP, w2, True, n, fresh=n == 0)
-            field[GMID, inner, columns(n)] = (slope[:, columns(n)] * value).astype(field.dtype)
-            send_halo(GMID, n)
+        def body(c):
+            at = place(c, width)
+            field[GMID, at[0], at[1]] = (slope[place(c)] * conv(GTOP, w2, True, c)).astype(field.dtype)
+            send_part(GMID, c)
+
+        run(GTOP, body)
 
     def step_low():
-        for c, (n, first, count) in enumerate(chunks):
-            at = (pl.ds(first, count), columns(n))
-            base = field[GTOP, pl.ds(width + first, count), columns(n)].astype(jnp.float32)
-            low[at] = (base + conv(GMID, w1, True, n, first, count, fresh=c == 0)).astype(low.dtype)
+        def body(c):
+            at = place(c, width)
+            base = field[GTOP, at[0], at[1]].astype(jnp.float32)
+            low[place(c)] = (base + conv(GMID, w1, True, c)).astype(low.dtype)
 
             @pl.when(jnp.logical_and(decoder, jnp.logical_not(middle)))
             def _():
@@ -256,22 +265,23 @@
             def _():
                 deliver(low, GRAD, c, at_prev).start()
 
-    pl.when(others)(lambda: step_hidden(first_tap))
-    pl.when(inner_dec)(lambda: step_pre(first_tap))
-    pl.when(encoder)(step_pre)
+        run(GMID, body)
+
+    load_w1.wait()
+    pl.when(others)(step_hidden)
+    pl.when(not_last)(step_pre)
     load_target.wait()
-    for a, b in taps:
-        load_tap(1, a, b).wait()
+    load_w2.wait()
     pl.when(others)(step_output)
     step_back()
+    pl.when(inner_dec)(step_hidden)
     step_low()
-    pl.when(inner_dec)(step_hidden)
     pl.when(inner_dec)(step_output)
 
     def drain(cond, src, kind, where, sent):
         @pl.when(cond)
         def _():
-            for c in range(len(chunks)):
+            for c in range(HALVES * HALVES):
                 copy = deliver(src, kind, c, where)
                 (copy.wait_send if sent else copy.wait_recv)()
 
@@ -325,7 +335,6 @@
     _, rows, width, channels = fwd_in.shape
     size = rows * width
     taps = w_first.shape[1] * w_first.shape[2]
-    chunks = ((0, 0, size), (1, 0, size // 2), (1, size // 2, size // 2))
     dtype = fwd_in.dtype
     sections = lax.axis_size("section")
     row_devices = lax.axis_size("rows")
@@ -336,7 +345,7 @@
     plane = pltpu.VMEM((size, channels), dtype)
     weight = pltpu.VMEM((taps, channels, channels), dtype)
     outs = pl.pallas_call(
-        functools.partial(relay_kernel, sections, row_devices, width, chunks),
+        functools.partial(relay_kernel, sections, row_devices, width),
         out_shape=[jax.ShapeDtypeStruct((size, channels), dtype)] * 3,
         in_specs=[hbm_spec] * 7,
         out_specs=[any_spec] * 3,
@@ -346,12 +355,11 @@
             pltpu.VMEM((5, size + 2 * width, channels), dtype),
             pltpu.VMEM((size, channels), jnp.float32),
             plane, plane,
-            pltpu.SemaphoreType.DMA((5,)),
-            pltpu.SemaphoreType.DMA((2, taps)),
+            pltpu.SemaphoreType.DMA((7,)),
             pltpu.SemaphoreType.DMA((5, 2, HALVES)),
             pltpu.SemaphoreType.DMA((5, 2, HALVES)),
-            pltpu.SemaphoreType.DMA((3, len(chunks))),
-            pltpu.SemaphoreType.DMA((3, len(chunks))),
+            pltpu.SemaphoreType.DMA((3, HALVES * HALVES)),
+            pltpu.SemaphoreType.DMA((3, HALVES * HALVES)),
         ],
         compiler_params=pltpu.CompilerParams(
             collective_id=0, has_side_effects=True, vmem_limit_bytes=62 * 2**20
@@ -369,7 +377,7 @@
     outs = pl.pallas_call(
         functools.partial(finish_kernel, sections, pieces),
         out_shape=[jax.ShapeDtypeStruct((size, channels), dtype)] * 3,
-        in_specs=[any_spec] * 3,
+        in_specs=[pl.BlockSpec(memory_space=pltpu.VMEM)] * 3,
         out_specs=[hbm_spec] * 3,
         scratch_shapes=[plane, pltpu.SemaphoreType.DMA((3, pieces))],
         compiler_params=pltpu.CompilerParams(vmem_limit_bytes=62 * 2**20),

time: 82.6 us -> 37 us (0.45)
  the two profiles are of different devices: /device:TPU:10 before, /device:TPU:0 now
where the time goes in v4:
time: 37 us; the launch traced here: 36.9 us
  Pallas kernels  36.3 us (98%)
  between operations  0.64 us (2%)
    pallas_call x1, Pallas kernels, on_device(): pl.pallas_call(functools.partial(relay_kernel, sections, row_devices, wid...  33.7 us
    pallas_call x1, Pallas kernels, on_device(): pl.pallas_call(functools.partial(finish_kernel, sections, pieces), out_sh...  2.58 us

profile of v4, /device:TPU:0, one launch (start us, length us, event | category | flops | bytes accessed | tf_op | source)
XLA Modules:
  0.0 36.9 jit_solution(8392218178653585137)
XLA Ops:
  0.6 33.7 %shard_map.94 = (bf16[512,512]{1,0:T(8,128)(2,1)}, bf16[512,512]{1,0:T(8,128)(2,1)}, bf16[512,512]{1,0:T(8,128)(2,1)}) custom-call(bf16[512,512]{1,0:T(8,128)(2,1)} %bitcast.12, bf16[512,512]{1,0:T(8,128)(2,1)} %bitcast.13, bf16[512,512]{1,0:T(8,128)(2,1)} %bitcast.14, bf16[512,512]{1,0:T(8,128)(2,1)} %bitcast.15, bf16[512,512]{1,0:T(8,128)(2,1)} %bitcast.16, ...), custom_call_target="tpu_custom_call" | custom-call | flops 12079595520 | bytes 13631488 | tf_op jit(solution)/shard_map/pallas_call | solution.py:347
  34.3 2.6 %shard_map.95 = (bf16[512,512]{1,0:T(8,128)(2,1)}, bf16[512,512]{1,0:T(8,128)(2,1)}, bf16[512,512]{1,0:T(8,128)(2,1)}) custom-call(bf16[512,512]{1,0:T(8,128)(2,1)} %get-tuple-element.9.fwd, bf16[512,512]{1,0:T(8,128)(2,1)} %get-tuple-element.10.grad, bf16[512,512]{1,0:T(8,128)(2,1)} %get-tuple-element.11.mirror), custom_call_target="tpu_custom_call" | custom-call | tf_op jit(solution)/shard_map/pallas_call | solution.py:377

commit v5 on v4

--- a/solution.py
+++ b/solution.py
@@ -55,9 +55,14 @@
     load_saved = load(saved_hbm, field.at[KEPT, inner], 3)
     load_target = load(target_hbm, target, 4)
 
-    load_w1 = load(w1_hbm, w1, 5)
-    load_w2 = load(w2_hbm, w2, 6)
-    for copy in (load_act, load_held, load_saved, load_w1, load_grad, load_target, load_w2):
+
+    def load_half(j, n):
+        src, dst = ((w1_hbm, w1), (w2_hbm, w2))[j]
+        cut = pl.ds(n * part, part)
+        return pltpu.make_async_copy(src.at[:, :, cut], dst.at[:, :, cut], in_sem.at[5 + HALVES * j + n])
+
+    for copy in (load_act, load_held, load_half(0, 0), load_saved, load_half(0, 1), load_grad, load_target,
+                 load_half(1, 0), load_half(1, 1)):
         copy.start()
 
     barrier = pltpu.get_barrier_semaphore()
@@ -111,13 +116,14 @@
         def _():
             halo_down(k, n).start()
 
-    def wait_halo(k):
+    def wait_top(k):
         @pl.when(has_up)
         def _():
             for n in range(HALVES):
                 halo_up(k, n).wait_send()
                 halo_down(k, n).wait_recv()
 
+    def wait_bottom(k):
         @pl.when(has_down)
         def _():
             for n in range(HALVES):
@@ -180,14 +186,32 @@
         right = jnp.where(column == width - 1, 0.0, pltpu.roll(right, tile - 1, 0))
         return left + centre + right
 
-    def run(k, body):
-        wait_halo(k)
-
-        def step(c, _):
-            body(c)
+    def run(k, body, turned, arrive=None):
+        def step(i, _):
+            n, m = i // HALVES, i % HALVES
+            if turned:
+                m = HALVES - 1 - m
+            if arrive is not None:
+                for h in range(HALVES):
+                    @pl.when(jnp.logical_and(arrive, i == HALVES * h))
+                    def _(h=h):
+                        load_half(0, h).wait()
+
+            @pl.when(i == int(turned))
+            def _():
+                wait_top(k)
+
+            @pl.when(i == int(not turned))
+            def _():
+                wait_bottom(k)
+
+            body(n * HALVES + m)
             return 0
 
         lax.fori_loop(0, HALVES * HALVES, step, 0)
+
+    def sigmoid(value):
+        return 0.5 + 0.5 * jnp.tanh(0.5 * value)
 
     def send_part(k, c):
         n, m = c // HALVES, c % HALVES
@@ -200,24 +224,24 @@
         def _():
             halo_down(k, n).start()
 
-    def step_hidden():
+    def step_hidden(arrive=None):
         def body(c):
             value = conv(U, w1, False, c)
-            sig = jax.nn.sigmoid(value)
+            sig = sigmoid(value)
             at = place(c, width)
             field[HID, at[0], at[1]] = (value * sig).astype(field.dtype)
             slope[place(c)] = sig * (1.0 + value * (1.0 - sig))
             send_part(HID, c)
 
-        run(U, body)
+        run(U, body, False, arrive)
 
     def step_pre():
         def body(c):
             value = conv(KEPT, w1, False, c)
-            sig = jax.nn.sigmoid(value)
+            sig = sigmoid(value)
             slope[place(c)] = sig * (1.0 + value * (1.0 - sig))
 
-        run(KEPT, body)
+        run(KEPT, body, False, inner_dec)
 
     def step_output():
         def body(c):
@@ -241,7 +265,7 @@
             def _():
                 deliver(y, FWD, c, at_next).start()
 
-        run(HID, body)
+        run(HID, body, True)
 
     def step_back():
         def body(c):
@@ -249,7 +273,7 @@
             field[GMID, at[0], at[1]] = (slope[place(c)] * conv(GTOP, w2, True, c)).astype(field.dtype)
             send_part(GMID, c)
 
-        run(GTOP, body)
+        run(GTOP, body, False)
 
     def step_low():
         def body(c):
@@ -265,13 +289,13 @@
             def _():
                 deliver(low, GRAD, c, at_prev).start()
 
-        run(GMID, body)
-
-    load_w1.wait()
-    pl.when(others)(step_hidden)
+        run(GMID, body, True)
+
+    pl.when(others)(lambda: step_hidden(others))
     pl.when(not_last)(step_pre)
     load_target.wait()
-    load_w2.wait()
+    for h in range(HALVES):
+        load_half(1, h).wait()
     pl.when(others)(step_output)
     step_back()
     pl.when(inner_dec)(step_hidden)
@@ -294,41 +318,54 @@
     drain(apart, y, MIRROR, at_mirror, True)
 
 
-def finish_kernel(sections, pieces, fwd, grad, mirror, fwd_out, grad_out, mirror_out, zeros, sem):
+def finish_kernel(sections, pieces, fwd, grad, mirror, fwd_out, grad_out, mirror_out, stage, in_sem, sem):
     section = lax.axis_index("section")
-    size = zeros.shape[0]
+    size = stage.shape[1]
     piece = size // pieces
     is_first, is_last = section == 0, section == sections - 1
     middle_enc = section == sections // 2 - 1
     middle_dec = section == sections // 2
+    has_prev, has_next = jnp.logical_not(is_first), jnp.logical_not(is_last)
     apart = jnp.logical_not(jnp.logical_or(middle_enc, middle_dec))
-    moves = (
-        (jnp.logical_not(is_first), fwd, fwd_out, 0),
-        (is_first, zeros, fwd_out, 0),
-        (jnp.logical_not(is_last), grad, grad_out, 1),
-        (is_last, zeros, grad_out, 1),
-        (middle_dec, fwd, mirror_out, 2),
-        (middle_enc, grad, mirror_out, 2),
-        (apart, mirror, mirror_out, 2),
-    )
-
-    def copies(src, dst, k):
-        for p in range(pieces):
-            rows = pl.ds(p * piece, piece)
-            yield pltpu.make_async_copy(src.at[rows], dst.at[rows], sem.at[k, p])
-
-    @pl.when(jnp.logical_or(is_first, is_last))
+    sources = ((has_prev, fwd, 0), (has_next, grad, 1), (apart, mirror, 2))
+
+    def fetch(src, k, p):
+        rows = pl.ds(p * piece, piece)
+        return pltpu.make_async_copy(src.at[rows], stage.at[k, rows], in_sem.at[k, p])
+
+    def put(k, dst, where, p):
+        rows = pl.ds(p * piece, piece)
+        return pltpu.make_async_copy(stage.at[k, rows], dst.at[rows], sem.at[where, p])
+
+    for p in range(pieces):
+        for cond, src, k in sources:
+            @pl.when(cond)
+            def _(src=src, k=k, p=p):
+                fetch(src, k, p).start()
+
+    @pl.when(is_first)
     def _():
-        zeros[...] = jnp.zeros_like(zeros)
-
-    for cond, src, dst, k in moves:
-        @pl.when(cond)
-        def _(src=src, dst=dst, k=k):
-            for copy in copies(src, dst, k):
-                copy.start()
-    for dst, k in ((fwd_out, 0), (grad_out, 1), (mirror_out, 2)):
-        for copy in copies(zeros, dst, k):
-            copy.wait()
+        stage[0] = jnp.zeros(stage.shape[1:], stage.dtype)
+
+    @pl.when(is_last)
+    def _():
+        stage[1] = jnp.zeros(stage.shape[1:], stage.dtype)
+
+    for p in range(pieces):
+        for cond, src, k in sources:
+            @pl.when(cond)
+            def _(src=src, k=k, p=p):
+                fetch(src, k, p).wait()
+        put(0, fwd_out, 0, p).start()
+        put(1, grad_out, 1, p).start()
+        for cond, k in ((middle_dec, 0), (middle_enc, 1), (apart, 2)):
+            @pl.when(cond)
+            def _(k=k, p=p):
+                put(k, mirror_out, 2, p).start()
+    for p in range(pieces):
+        put(0, fwd_out, 0, p).wait()
+        put(1, grad_out, 1, p).wait()
+        put(2, mirror_out, 2, p).wait()
 
 
 def on_device(fwd_in, grad_in, saved_in, mirror_held, target, w_first, w_second):
@@ -355,7 +392,7 @@
             pltpu.VMEM((5, size + 2 * width, channels), dtype),
             pltpu.VMEM((size, channels), jnp.float32),
             plane, plane,
-            pltpu.SemaphoreType.DMA((7,)),
+            pltpu.SemaphoreType.DMA((5 + 2 * HALVES,)),
             pltpu.SemaphoreType.DMA((5, 2, HALVES)),
             pltpu.SemaphoreType.DMA((5, 2, HALVES)),
             pltpu.SemaphoreType.DMA((3, HALVES * HALVES)),
@@ -373,13 +410,17 @@
         flat(fwd_in), flat(grad_in), flat(saved_in), flat(mirror_held), flat(target),
         flat_w(w_first), flat_w(w_second),
     )
-    pieces = 2
+    pieces = 4
     outs = pl.pallas_call(
         functools.partial(finish_kernel, sections, pieces),
         out_shape=[jax.ShapeDtypeStruct((size, channels), dtype)] * 3,
-        in_specs=[pl.BlockSpec(memory_space=pltpu.VMEM)] * 3,
+        in_specs=[any_spec] * 3,
         out_specs=[hbm_spec] * 3,
-        scratch_shapes=[plane, pltpu.SemaphoreType.DMA((3, pieces))],
+        scratch_shapes=[
+            pltpu.VMEM((3, size, channels), dtype),
+            pltpu.SemaphoreType.DMA((3, pieces)),
+            pltpu.SemaphoreType.DMA((3, pieces)),
+        ],
         compiler_params=pltpu.CompilerParams(vmem_limit_bytes=62 * 2**20),
     )(*outs)
     return tuple(value.reshape(fwd_in.shape) for value in outs)

time: 37 us -> 36.5 us (0.986)
  Pallas kernels: 36.3 us -> 35.7 us
where the time goes in v5:
time: 36.5 us; the launch traced here: 36.3 us
  Pallas kernels  35.7 us (98%)
  between operations  0.64 us (2%)
    pallas_call x1, Pallas kernels, on_device(): pl.pallas_call(functools.partial(relay_kernel, sections, row_devices, wid...  33.4 us
    pallas_call x1, Pallas kernels, on_device(): pl.pallas_call(functools.partial(finish_kernel, sections, pieces), out_sh...  2.31 us

profile of v5, /device:TPU:0, one launch (start us, length us, event | category | flops | bytes accessed | tf_op | source)
XLA Modules:
  0.0 36.3 jit_solution(5552507751897157860)
XLA Ops:
  0.6 33.4 %shard_map.94 = (bf16[512,512]{1,0:T(8,128)(2,1)}, bf16[512,512]{1,0:T(8,128)(2,1)}, bf16[512,512]{1,0:T(8,128)(2,1)}) custom-call(bf16[512,512]{1,0:T(8,128)(2,1)} %bitcast.12, bf16[512,512]{1,0:T(8,128)(2,1)} %bitcast.13, bf16[512,512]{1,0:T(8,128)(2,1)} %bitcast.14, bf16[512,512]{1,0:T(8,128)(2,1)} %bitcast.15, bf16[512,512]{1,0:T(8,128)(2,1)} %bitcast.16, ...), custom_call_target="tpu_custom_call" | custom-call | flops 12079595520 | bytes 13631488 | tf_op jit(solution)/shard_map/pallas_call | solution.py:384
  34.0 2.3 %shard_map.95 = (bf16[512,512]{1,0:T(8,128)(2,1)}, bf16[512,512]{1,0:T(8,128)(2,1)}, bf16[512,512]{1,0:T(8,128)(2,1)}) custom-call(bf16[512,512]{1,0:T(8,128)(2,1)} %get-tuple-element.9.fwd, bf16[512,512]{1,0:T(8,128)(2,1)} %get-tuple-element.10.grad, bf16[512,512]{1,0:T(8,128)(2,1)} %get-tuple-element.11.mirror), custom_call_target="tpu_custom_call" | custom-call | tf_op jit(solution)/shard_map/pallas_call | solution.py:414
